TPU v7x, 32 devices: a whole 2x2x4 slice. The times are simulated.
32 devices in a mesh: layer: 8 (over z, core), dp: 2 (over y), mp: 2 (over x).
Axes of the slice: x: 2, y: 2, z: 4, core: 2. Of those that a mesh axis runs over, the one named last changes fastest.
Arguments:
- states: bfloat16 [32, 256, 1024], P('layer', 'dp'), may hold values from -6 to 6
- weights: bfloat16 [32, 1024, 1024], P('layer', 'dp', 'mp'), may hold values from -0.1875 to 0.1875
- guess_points: bfloat16 [8, 256, 1024], P('layer', 'dp'), may hold values from -2 to 2
- cotangent: bfloat16 [256, 1024], P('dp'), may hold values from -6 to 6
Outputs:
- adjoint: bfloat16 [32, 256, 1024], P('layer', 'dp', 'mp')
- weight_grads: float32 [32, 1024, 1024], P('layer', 'dp', 'mp')
All inputs are finite; a program needn't handle non-finite values.
Results may differ from a plain program's by a relative error of at most 0.03.
Values may be sent and summed in bfloat16 or wider, within the bound.
A program may use at most 64 MiB of HBM per device.

v0:
```python
import jax
import jax.numpy as jnp
from jax import lax
from jax.sharding import PartitionSpec as P

step_size = 0.1


def from_behind(value, axis, steps):
    count = lax.axis_size(axis)
    leading, last = (max(0, -steps), min(count, count - steps))
    return lax.ppermute(value, axis, [(source, source + steps) for source in range(leading, last)])


def shortened(array):
    return jax.tree.map(lambda a: a.astype(jnp.bfloat16) if a.dtype == jnp.float32 else a, array)


def slope_of(inputs, weight_block):
    tangent = jnp.tanh(jnp.dot(inputs, weight_block, preferred_element_type=jnp.float32))
    return 1.0 - tangent * tangent


def back_product(scaled_rows, weight_block):
    return lax.dot_general(
        scaled_rows, weight_block, (((1,), (1,)), ((), ())), preferred_element_type=jnp.float32
    )


def body(states, weights, guess_points, cotangent):
    slab_count = lax.axis_size("layer")
    slab_index = lax.axis_index("layer")
    half_index = lax.axis_index("mp")
    layer_count, row_count, model_width = states.shape
    point_count = guess_points.shape[0]
    factor = layer_count // point_count
    columns = weights.shape[2]
    half_rows = row_count // lax.axis_size("mp")
    row_start = half_index * half_rows
    col_start = half_index * columns
    gathered = lax.all_gather(weights, "dp", axis=1, tiled=True)
    next_point = from_behind(guess_points[0], "layer", -1)
    terminal = jnp.where(
        slab_index == slab_count - 1, cotangent.astype(jnp.float32), next_point.astype(jnp.float32)
    )
    guess_wide = guess_points.astype(jnp.float32)
    slopes = [slope_of(states[layer_id], gathered[layer_id]) for layer_id in range(layer_count)]

    def scale_columns(upper_adj, layer_id):
        own_part = lax.dynamic_slice_in_dim(upper_adj, col_start, columns, 1)
        return (own_part * slopes[layer_id]).astype(jnp.bfloat16)

    def fine_step(upper_adj, scaled_rows, layer_id):
        summed = lax.psum(back_product(scaled_rows, gathered[layer_id]), "mp")
        return upper_adj + step_size * summed

    upper_adj = terminal
    residuals = [None] * point_count
    for layer_id in range(layer_count - 1, -1, -1):
        relaxed = fine_step(upper_adj, scale_columns(upper_adj, layer_id), layer_id)
        if layer_id % factor == 0:
            residuals[layer_id // factor] = relaxed - guess_wide[layer_id // factor]
            upper_adj = guess_wide[layer_id // factor]
        else:
            upper_adj = relaxed
    residual_half = lax.dynamic_slice_in_dim(jnp.stack(residuals), row_start, half_rows, 1)
    coarse_weights = lax.all_gather(gathered[::factor], "mp", axis=2, tiled=True)
    state_half = lax.dynamic_slice_in_dim(states[::factor], row_start, half_rows, 1)
    coarse_slopes = jnp.stack([slope_of(state_half[0], coarse_weights[0])])

    def coarse_solve(incoming):
        carried = incoming.astype(jnp.float32)
        results = [None] * point_count
        scaled_rows = (carried * coarse_slopes[0]).astype(jnp.bfloat16)
        stepped = (
            carried
            + factor * step_size * back_product(scaled_rows, coarse_weights[0])
            + residual_half[0]
        )
        results[0] = stepped.astype(jnp.bfloat16)
        return jnp.stack(results)

    def solve_pair(operand_pair):
        return coarse_solve(operand_pair[0])

    def keep_pair(operand_pair):
        return operand_pair[1]

    def one_turn(turn_id, loop_state):
        incoming, errors = loop_state
        errors = lax.cond(
            turn_id == slab_count - 1 - slab_index, solve_pair, keep_pair, (incoming, errors)
        )
        incoming = from_behind(shortened(errors[0]), "layer", -1)
        return (incoming, errors)

    start_in = jnp.zeros((half_rows, model_width), jnp.bfloat16)
    start_errors = jnp.zeros((point_count, half_rows, model_width), jnp.bfloat16)
    incoming, errors = lax.fori_loop(0, slab_count - 1, one_turn, (start_in, start_errors))
    errors = lax.cond(slab_index == 0, solve_pair, keep_pair, (incoming, errors))
    adjoint_parts = [None] * layer_count
    scaled_parts = [None] * layer_count
    spread = lax.all_gather(
        shortened(jnp.concatenate([errors, incoming[None]], 0)), "mp", axis=1, tiled=True
    )
    upper_adj = terminal + spread[point_count].astype(jnp.float32)
    for layer_id in range(layer_count - 1, -1, -1):
        scaled_rows = scale_columns(upper_adj, layer_id)
        if layer_id % factor == 0:
            current = guess_wide[layer_id // factor] + spread[layer_id // factor].astype(
                jnp.float32
            )
        else:
            current = fine_step(upper_adj, scaled_rows, layer_id)
        adjoint_parts[layer_id] = lax.dynamic_slice_in_dim(current, col_start, columns, 1).astype(
            jnp.bfloat16
        )
        scaled_parts[layer_id] = scaled_rows
        upper_adj = current
    adjoint_out = jnp.stack(adjoint_parts)
    scaled_out = jnp.stack(scaled_parts)
    partial_terms = jnp.einsum(
        "lrd,lrh->ldh", states, scaled_out, preferred_element_type=jnp.float32
    )
    weight_grads = step_size * lax.psum_scatter(
        partial_terms.astype(jnp.bfloat16), "dp", scatter_dimension=1, tiled=True
    ).astype(jnp.float32)
    return (adjoint_out, weight_grads)


def solution(mesh):
    return jax.shard_map(
        body,
        mesh=mesh,
        in_specs=(
            P("layer", "dp", None),
            P("layer", "dp", "mp"),
            P("layer", "dp", None),
            P("dp", None),
        ),
        out_specs=(P("layer", "dp", "mp"), P("layer", "dp", "mp")),
        check_vma=False,
    )
```

profile of v0, /device:TPU:0, one launch (start us, length us, event | category | flops | bytes accessed | tf_op | source)
XLA Modules:
  0.0 466.0 jit_solution(16971392643155577218)
XLA Ops:
  12.6 56.4 %all-gather.3.cloned.1.call-done = bf16[4,1024,512]{2,1,0:T(8,128)(2,1)} async-done(((bf16[4,512,512]{2,1,0:T(8,128)(2,1)}), bf16[4,1024,512]{2,1,0:T(8,128)(2,1)}) %all-gather.3.cloned.1.call-update) | async-done | bytes 4194320 | tf_op jit(solution)/shard_map/all_gather | solution.py:41
  75.5 27.1 %all-reduce.8.cloned.1.call-done = f32[128,1024]{1,0:T(8,128)} async-done(((f32[128,1024]{1,0:T(8,128)}), f32[128,1024]{1,0:T(8,128)}) %all-reduce.8.cloned.1.call-update) | async-done | bytes 524304 | tf_op jit(solution)/shard_map/psum | solution.py:54
  103.7 2.5 fusion.63
  107.9 27.1 %all-reduce.10.cloned.1.call-done = f32[128,1024]{1,0:T(8,128)} async-done(((f32[128,1024]{1,0:T(8,128)}), f32[128,1024]{1,0:T(8,128)}) %all-reduce.10.cloned.1.call-update) | async-done | bytes 524304 | tf_op jit(solution)/shard_map/psum | solution.py:54
  136.1 2.5 fusion.65
  140.3 27.1 %all-reduce.12.cloned.1.call-done = f32[128,1024]{1,0:T(8,128)} async-done(((f32[128,1024]{1,0:T(8,128)}), f32[128,1024]{1,0:T(8,128)}) %all-reduce.12.cloned.1.call-update) | async-done | bytes 524304 | tf_op jit(solution)/shard_map/psum | solution.py:54
  168.5 2.5 fusion.57
  174.5 25.3 %all-reduce.14.cloned.1.call-done = f32[128,1024]{1,0:T(8,128)} async-done(((f32[128,1024]{1,0:T(8,128)}), f32[128,1024]{1,0:T(8,128)}) %all-reduce.14.cloned.1.call-update) | async-done | bytes 524304 | tf_op jit(solution)/shard_map/psum | solution.py:54
  200.8 34.1 %all-gather.5.cloned.1.call-done = bf16[1,1024,1024]{2,1,0:T(8,128)(2,1)} async-done(((bf16[1,1024,512]{2,1,0:T(8,128)(2,1)}), bf16[1,1024,1024]{2,1,0:T(8,128)(2,1)}) %all-gather.5.cloned.1.call-update) | async-done | bytes 2097168 | tf_op jit(solution)/shard_map/all_gather | solution.py:67
  237.1 45.3 %while.23 = (s32[]{:T(128)}, bf16[64,1024]{1,0:T(8,128)(2,1)S(1)}, bf16[1,64,1024]{2,1,0:T(8,128)(2,1)S(1)}, s32[]{:T(128)}, f32[64,1024]{1,0:T(8,128)S(1)}, /*i...) while((s32[]{:T(128)}, bf16[64,1024]{1,0:T(8,128)(2,1)S(1)}, ...), condition=%wide.region_7.8_spmd, body=%wide.region_4.7_spmd.sunk | while | flops 134742016 | bytes 3408051 | solution.py:99
  241.7 4.4 collective-permute-done
  247.3 5.0 %collective-permute-done = bf16[64,1024]{1,0:T(8,128)(2,1)S(1)} collective-permute-done((bf16[64,1024]{1,0:T(8,128)(2,1)S(1)}, bf16[64,1024]{1,0:T(8,128)(2,1)S(1)}, u32[]{:S(2)}, u32[]{:S(2)}) %collective-permute-start) | collective-permute-done | bytes 131104 | tf_op jit(solution)/shard_map/while/body/eval_jaxpr/ppermute | solution.py:12
  253.6 5.0 %collective-permute-done = bf16[64,1024]{1,0:T(8,128)(2,1)S(1)} collective-permute-done((bf16[64,1024]{1,0:T(8,128)(2,1)S(1)}, bf16[64,1024]{1,0:T(8,128)(2,1)S(1)}, u32[]{:S(2)}, u32[]{:S(2)}) %collective-permute-start) | collective-permute-done | bytes 131104 | tf_op jit(solution)/shard_map/while/body/eval_jaxpr/ppermute | solution.py:12
  259.9 5.0 %collective-permute-done = bf16[64,1024]{1,0:T(8,128)(2,1)S(1)} collective-permute-done((bf16[64,1024]{1,0:T(8,128)(2,1)S(1)}, bf16[64,1024]{1,0:T(8,128)(2,1)S(1)}, u32[]{:S(2)}, u32[]{:S(2)}) %collective-permute-start) | collective-permute-done | bytes 131104 | tf_op jit(solution)/shard_map/while/body/eval_jaxpr/ppermute | solution.py:12
  266.2 5.0 %collective-permute-done = bf16[64,1024]{1,0:T(8,128)(2,1)S(1)} collective-permute-done((bf16[64,1024]{1,0:T(8,128)(2,1)S(1)}, bf16[64,1024]{1,0:T(8,128)(2,1)S(1)}, u32[]{:S(2)}, u32[]{:S(2)}) %collective-permute-start) | collective-permute-done | bytes 131104 | tf_op jit(solution)/shard_map/while/body/eval_jaxpr/ppermute | solution.py:12
  272.4 10.0 %collective-permute-done = bf16[64,1024]{1,0:T(8,128)(2,1)S(1)} collective-permute-done((bf16[64,1024]{1,0:T(8,128)(2,1)S(1)}, bf16[64,1024]{1,0:T(8,128)(2,1)S(1)}, u32[]{:S(2)}, u32[]{:S(2)}) %collective-permute-start) | collective-permute-done | bytes 131104 | tf_op jit(solution)/shard_map/while/body/eval_jaxpr/ppermute | solution.py:12
  284.8 9.6 %all_gather.11 = bf16[2,128,1024]{2,1,0:T(8,128)(2,1)S(1)} all-gather(bf16[2,64,1024]{2,1,0:T(8,128)(2,1)S(1)} %pad_maximum_fusion.1), channel_id=1, replica_groups=mesh['layer'=8,'dp'=2,'mp'=2] {'mp'}, dimensions={1}, use_global_device_ids=true | all-gather | bytes 786432 | tf_op jit(solution)/shard_map/all_gather | solution.py:103
  297.1 26.4 %all-reduce.16.cloned.1.call-done = f32[128,1024]{1,0:T(8,128)} async-done(((f32[128,1024]{1,0:T(8,128)}), f32[128,1024]{1,0:T(8,128)}) %all-reduce.16.cloned.1.call-update) | async-done | bytes 524304 | tf_op jit(solution)/shard_map/psum | solution.py:54
  328.2 28.7 %all-reduce.18.cloned.1.call-done = f32[128,1024]{1,0:T(8,128)} async-done(((f32[128,1024]{1,0:T(8,128)}), f32[128,1024]{1,0:T(8,128)}) %all-reduce.18.cloned.1.call-update) | async-done | bytes 524304 | tf_op jit(solution)/shard_map/psum | solution.py:54
  361.5 28.7 %all-reduce.20.cloned.1.call-done = f32[128,1024]{1,0:T(8,128)} async-done(((f32[128,1024]{1,0:T(8,128)}), f32[128,1024]{1,0:T(8,128)}) %all-reduce.20.cloned.1.call-update) | async-done | bytes 524304 | tf_op jit(solution)/shard_map/psum | solution.py:54
  392.0 3.3 convert_bitcast_fusion
  397.1 52.7 %reduce-scatter.2.cloned.1.call-done = bf16[4,512,512]{1,2,0:T(8,128)(2,1)} async-done(((bf16[4,1024,512]{1,2,0:T(8,128)(2,1)}), bf16[4,512,512]{1,2,0:T(8,128)(2,1)}) %reduce-scatter.2.cloned.1.call-update) | async-done | bytes 2097168 | tf_op jit(solution)/shard_map/reduce_scatter | solution.py:125
  449.8 4.2 convert_multiply_fusion.2
  453.9 5.2 %copy.7 = f32[4,512,512]{2,1,0:T(8,128)} copy(f32[4,512,512]{1,2,0:T(8,128)} %convert_multiply_fusion.2) | data formatting | bytes 8388608
  (86 shorter events, 56.0 us)
Async XLA Ops:
  7.2 66.8 %copy-start = (bf16[4,128,1024]{2,1,0:T(8,128)(2,1)S(1)}, bf16[4,128,1024]{2,1,0:T(8,128)(2,1)}, u32[]{:S(2)}) copy-start(bf16[4,128,1024]{2,1,0:T(8,128)(2,1)} %param.10) | copy-start | bytes 3145732
  7.2 61.9 %all-gather.3.cloned.1.call-start = ((), (), s32[]{:S(2)}) async-start(), calls=%async_computation.1 | async-start | bytes 6291456 | tf_op jit(solution)/shard_map/all_gather | solution.py:41
  7.9 94.7 %all-reduce.8.cloned.1.call-start = ((), (), s32[]{:S(2)}) async-start(), calls=%async_computation.3 | async-start | bytes 1048576 | tf_op jit(solution)/shard_map/psum | solution.py:54
  8.0 3.6 collective-permute-start.1
  73.9 61.1 %all-reduce.10.cloned.1.call-start = ((), (), s32[]{:S(2)}) async-start(), calls=%async_computation.4 | async-start | bytes 1048576 | tf_op jit(solution)/shard_map/psum | solution.py:54
  75.5 32.4 %copy-start.2 = (f32[128,512]{1,0:T(8,128)}, f32[128,512]{1,0:T(8,128)S(1)}, u32[]{:S(2)}) copy-start(f32[128,512]{1,0:T(8,128)S(1)} %fusion.54) | copy-start | bytes 786436
  106.3 61.1 %all-reduce.12.cloned.1.call-start = ((), (), s32[]{:S(2)}) async-start(), calls=%async_computation.5 | async-start | bytes 1048576 | tf_op jit(solution)/shard_map/psum | solution.py:54
  107.9 63.2 %copy-start.1 = (f32[128,512]{1,0:T(8,128)}, f32[128,512]{1,0:T(8,128)S(1)}, u32[]{:S(2)}) copy-start(f32[128,512]{1,0:T(8,128)S(1)} %fusion.55) | copy-start | bytes 786436
  138.7 61.2 %all-reduce.14.cloned.1.call-start = ((), (), s32[]{:S(2)}) async-start(), calls=%async_computation.6 | async-start | bytes 1048576 | tf_op jit(solution)/shard_map/psum | solution.py:54
  140.3 33.2 %copy-start.5 = (f32[128,512]{1,0:T(8,128)}, f32[128,512]{1,0:T(8,128)S(1)}, u32[]{:S(2)}) copy-start(f32[128,512]{1,0:T(8,128)S(1)} %fusion.56) | copy-start | bytes 786436
  168.5 66.5 %slice-start = ((bf16[4,128,1024]{2,1,0:T(8,128)(2,1)}), bf16[1,128,1024]{2,1,0:T(8,128)(2,1)S(1)}, s32[]{:S(2)}) async-start(bf16[4,128,1024]{2,1,0:T(8,128)(2,1)} %param.10), calls=%async_computation.11 | async-start | bytes 524288 | tf_op jit(solution)/shard_map/slice | solution.py:68
  171.1 63.9 %all-gather.5.cloned.1.call-start = ((), (), s32[]{:S(2)}) async-start(), calls=%async_computation.2 | async-start | bytes 3145728 | tf_op jit(solution)/shard_map/all_gather | solution.py:67
  173.4 150.1 %all-reduce.16.cloned.1.call-start = ((), (), s32[]{:S(2)}) async-start(), calls=%async_computation.7 | async-start | bytes 1048576 | tf_op jit(solution)/shard_map/psum | solution.py:54
  237.1 3.2 collective-permute-start
  240.4 5.6 %collective-permute-start = (bf16[64,1024]{1,0:T(8,128)(2,1)S(1)}, bf16[64,1024]{1,0:T(8,128)(2,1)S(1)}, u32[]{:S(2)}, u32[]{:S(2)}) collective-permute-start(bf16[64,1024]{1,0:T(8,128)(2,1)S(1)} %bitcast.117), channel_id=1, source_target_pairs={{4,0},{8,4},{12,8},{16,12},{20,16},{24,20},{28,24},{5,1},{9,5},{13... | collective-permute-start | bytes 393224 | tf_op jit(solution)/shard_map/while/body/eval_jaxpr/ppermute | solution.py:12
  246.0 6.3 %collective-permute-start = (bf16[64,1024]{1,0:T(8,128)(2,1)S(1)}, bf16[64,1024]{1,0:T(8,128)(2,1)S(1)}, u32[]{:S(2)}, u32[]{:S(2)}) collective-permute-start(bf16[64,1024]{1,0:T(8,128)(2,1)S(1)} %bitcast.117), channel_id=1, source_target_pairs={{4,0},{8,4},{12,8},{16,12},{20,16},{24,20},{28,24},{5,1},{9,5},{13... | collective-permute-start | bytes 393224 | tf_op jit(solution)/shard_map/while/body/eval_jaxpr/ppermute | solution.py:12
  252.3 6.3 %collective-permute-start = (bf16[64,1024]{1,0:T(8,128)(2,1)S(1)}, bf16[64,1024]{1,0:T(8,128)(2,1)S(1)}, u32[]{:S(2)}, u32[]{:S(2)}) collective-permute-start(bf16[64,1024]{1,0:T(8,128)(2,1)S(1)} %bitcast.117), channel_id=1, source_target_pairs={{4,0},{8,4},{12,8},{16,12},{20,16},{24,20},{28,24},{5,1},{9,5},{13... | collective-permute-start | bytes 393224 | tf_op jit(solution)/shard_map/while/body/eval_jaxpr/ppermute | solution.py:12
  258.6 6.3 %collective-permute-start = (bf16[64,1024]{1,0:T(8,128)(2,1)S(1)}, bf16[64,1024]{1,0:T(8,128)(2,1)S(1)}, u32[]{:S(2)}, u32[]{:S(2)}) collective-permute-start(bf16[64,1024]{1,0:T(8,128)(2,1)S(1)} %bitcast.117), channel_id=1, source_target_pairs={{4,0},{8,4},{12,8},{16,12},{20,16},{24,20},{28,24},{5,1},{9,5},{13... | collective-permute-start | bytes 393224 | tf_op jit(solution)/shard_map/while/body/eval_jaxpr/ppermute | solution.py:12
  264.9 6.3 %collective-permute-start = (bf16[64,1024]{1,0:T(8,128)(2,1)S(1)}, bf16[64,1024]{1,0:T(8,128)(2,1)S(1)}, u32[]{:S(2)}, u32[]{:S(2)}) collective-permute-start(bf16[64,1024]{1,0:T(8,128)(2,1)S(1)} %bitcast.117), channel_id=1, source_target_pairs={{4,0},{8,4},{12,8},{16,12},{20,16},{24,20},{28,24},{5,1},{9,5},{13... | collective-permute-start | bytes 393224 | tf_op jit(solution)/shard_map/while/body/eval_jaxpr/ppermute | solution.py:12
  271.1 11.3 %collective-permute-start = (bf16[64,1024]{1,0:T(8,128)(2,1)S(1)}, bf16[64,1024]{1,0:T(8,128)(2,1)S(1)}, u32[]{:S(2)}, u32[]{:S(2)}) collective-permute-start(bf16[64,1024]{1,0:T(8,128)(2,1)S(1)} %bitcast.117), channel_id=1, source_target_pairs={{4,0},{8,4},{12,8},{16,12},{20,16},{24,20},{28,24},{5,1},{9,5},{13... | collective-permute-start | bytes 393224 | tf_op jit(solution)/shard_map/while/body/eval_jaxpr/ppermute | solution.py:12
  282.4 12.1 %copy-start.4 = (f32[128,512]{1,0:T(8,128)S(1)}, f32[128,512]{1,0:T(8,128)}, u32[]{:S(2)}) copy-start(f32[128,512]{1,0:T(8,128)} %copy-done.3) | copy-start | bytes 786436
  297.0 59.8 %all-reduce.18.cloned.1.call-start = ((), (), s32[]{:S(2)}) async-start(), calls=%async_computation.8 | async-start | bytes 1048576 | tf_op jit(solution)/shard_map/psum | solution.py:54
  328.1 62.1 %all-reduce.20.cloned.1.call-start = ((), (), s32[]{:S(2)}) async-start(), calls=%async_computation.9 | async-start | bytes 1048576 | tf_op jit(solution)/shard_map/psum | solution.py:54
  361.5 88.3 %reduce-scatter.2.cloned.1.call-start = ((), (), s32[]{:S(2)}) async-start(), calls=%async_computation.10 | async-start | bytes 6291456 | tf_op jit(solution)/shard_map/reduce_scatter | solution.py:125
  (2 other events, 1.6 us)
Sparse Core Ops, SparseCore 0:
  9.6 59.4 all-gather.2
  74.0 28.5 all-reduce.7
  106.4 28.5 all-reduce.9
  138.8 28.5 all-reduce.11
  171.2 28.5 all-reduce.13
  201.8 33.1 all-gather.4
  297.2 26.2 all-reduce.15
  328.2 28.5 all-reduce.17
  361.6 28.5 all-reduce.19
  395.4 54.3 reduce-scatter.1
where the time goes:
time: 467 us; the launch traced here: 466 us
  waiting for transfers between devices  373 us (80%)
  matrix products  31.6 us (7%)
  other arithmetic  17.4 us (4%)
  between operations  14.4 us (3%)
  starting transfers between devices  10.7 us (2%)
  blocking collectives  9.56 us (2%)
  local copies, waits for them, and re-layouts  9.03 us (2%)
    psum x7, waiting for transfers between devices, fine_step(): summed = lax.psum(back_product(scaled_rows, gathered[layer_id]), 'mp')  191 us
    all_gather x1, waiting for transfers between devices, body(): gathered = lax.all_gather(weights, 'dp', axis=1, tiled=True)  56.4 us
    reduce_scatter x1, waiting for transfers between devices, body(): lax.psum_scatter(partial_terms.astype(jnp.bfloat16), 'dp', scatter_dimens...  52.7 us
    ppermute x8, waiting for transfers between devices, from_behind(): lax.ppermute(value, axis, [(source, source + steps) for source in range(l...  38.5 us
    all_gather x1, waiting for transfers between devices, body(): lax.all_gather(gathered[::factor], 'mp', axis=2, tiled=True)  34.1 us
    dot_general x8, matrix products, back_product(): lax.dot_general(scaled_rows, weight_block, (((1,), (1,)), ((), ())), pref...  19.9 us
    ppermute x8, starting transfers between devices, from_behind(): lax.ppermute(value, axis, [(source, source + steps) for source in range(l...  10.3 us
    all_gather x1, blocking collectives, body(): lax.all_gather(shortened(jnp.concatenate([errors, incoming[None]], 0)), '...  9.56 us
  transfers between devices with their start and end apart: 18, of which 18 were waited for; matrix products, arithmetic and copies ran while one was open for 2% of the time, Pallas kernels for 0%

commit v1 on v0

v1 whole, which is shorter than its diff:
```python
import functools

import jax
import jax.numpy as jnp
from jax import lax
from jax.experimental import pallas as pl
from jax.experimental.pallas import tpu as pltpu
from jax.sharding import PartitionSpec as P

step_size = 0.1
f32, bf16 = jnp.float32, jnp.bfloat16
MESH = pl.DeviceIdType.MESH


def back_product(scaled_rows, weight_block):
    return lax.dot_general(
        scaled_rows, weight_block, (((1,), (1,)), ((), ())), preferred_element_type=f32
    )


def slope_of(inputs, weight_block):
    tangent = jnp.tanh(jnp.dot(inputs, weight_block, preferred_element_type=f32))
    return 1.0 - tangent * tangent


def cycle(
    slab_count, dp_count, layers,
    states, weights, guess, cotangent, adjoint, grads,
    gw, cw, npt, slopes, cslopes, vbuf, sbuf, terminal,
    exs, exr, r0s, r0r, resid, inc, oinc, ebuf, oe, sg, stg, stt,
    wsend, wrecv, csend, crecv, lsem, ssend, srecv, gsend, grecv,
    xsend, xrecv, nsend, nrecv, hsend, hrecv,
):
    slab, mine, j = lax.axis_index("layer"), lax.axis_index("dp"), lax.axis_index("mp")
    o = 1 - j
    rows, width = states.shape[1], states.shape[2]
    blk, cols = weights.shape[1], weights.shape[2]
    half = rows // 2
    peers = range(1, dp_count)
    to_peer = [lax.rem(mine + d, dp_count) for d in peers]
    from_peer = [lax.rem(mine + dp_count - d, dp_count) for d in peers]
    not_top, not_low = slab < slab_count - 1, slab > 0
    own_in = pl.ds(pl.multiple_of(mine * blk, blk), blk)
    own_rows = pl.ds(pl.multiple_of(mine * rows, rows), rows)
    half_j = pl.ds(pl.multiple_of(j * half, half), half)
    half_o = pl.ds(pl.multiple_of(o * half, half), half)
    cols_j = pl.ds(pl.multiple_of(j * cols, cols), cols)
    cols_o = pl.ds(pl.multiple_of(o * cols, cols), cols)

    def remote(src, dst, send, recv, device):
        return pltpu.make_async_remote_copy(
            src_ref=src, dst_ref=dst, send_sem=send, recv_sem=recv,
            device_id=device, device_id_type=MESH,
        )

    barrier = pltpu.get_barrier_semaphore()

    def greet(device):
        pl.semaphore_signal(barrier, inc=1, device_id=device, device_id_type=MESH)

    for peer in to_peer:
        greet({"dp": peer})
    greet({"mp": o})

    @pl.when(not_top)
    def _():
        greet({"layer": slab + 1})

    @pl.when(not_low)
    def _():
        greet({"layer": slab - 1})

    pl.semaphore_wait(
        barrier, dp_count + not_top.astype(jnp.int32) + not_low.astype(jnp.int32)
    )

    def home(layer):
        return cw.at[j] if layer == 0 else gw.at[layer - 1]

    partner = {"mp": o}
    point_copy = remote(guess.at[0, :, cols_j], npt, nsend.at[0], nrecv.at[0], {"layer": slab - 1})

    @pl.when(not_low)
    def _():
        point_copy.start()

    w_copies, local_copies = {}, {}
    c_copies = [remote(weights.at[0], cw.at[j, own_in], csend.at[0], crecv.at[0], partner)]
    c_copies[0].start()
    order = [0] + list(range(layers - 1, 0, -1))
    for layer in order:
        for d in peers:
            w_copies[layer, d] = remote(
                weights.at[layer], home(layer).at[own_in],
                wsend.at[layer, d - 1], wrecv.at[layer, d - 1], {"dp": to_peer[d - 1]},
            )
            w_copies[layer, d].start()
    for layer in order:
        local_copies[layer] = pltpu.make_async_copy(
            weights.at[layer], home(layer).at[own_in], lsem.at[layer]
        )
        local_copies[layer].start()

    @pl.when(not_top)
    def _():
        point_copy.wait_recv()
        terminal[...] = npt[...].astype(f32)

    @pl.when(jnp.logical_not(not_top))
    def _():
        terminal[...] = cotangent[:, cols_j].astype(f32)

    local_copies[0].wait()
    for d in peers:
        w_copies[0, d].wait_recv()
        block = pl.ds(pl.multiple_of(from_peer[d - 1] * blk, blk), blk)
        c_copies.append(
            remote(cw.at[j, block], cw.at[j, block], csend.at[d], crecv.at[d], partner)
        )
        c_copies[d].start()
    slopes[0] = slope_of(states[0], cw[j])

    pending = []

    def exchange_step(slot, layer, v, s, between=None):
        w = home(layer)
        exs[slot] = (step_size * back_product(s, w[cols_o, :])).astype(bf16)
        copy = remote(exs.at[slot], exr.at[slot], xsend.at[slot], xrecv.at[slot], partner)
        copy.start()
        pending.append(copy)
        v = v + step_size * back_product(s, w[cols_j, :])
        if between is not None:
            between()
        copy.wait_recv()
        return v + exr[slot].astype(f32)

    v = terminal[...]
    slot = 0
    for layer in range(layers - 1, 0, -1):
        local_copies[layer].wait()
        for d in peers:
            w_copies[layer, d].wait_recv()
        slopes[layer] = slope_of(states[layer], gw[layer - 1])
        s = (v * slopes[layer]).astype(bf16)
        v = exchange_step(slot, layer, v, s)
        slot += 1
    vbuf[...] = v
    sbuf[...] = (v * slopes[0]).astype(bf16)
    s_far = sbuf[half_o, :]
    for c in range(2):
        far = step_size * back_product(s_far, cw[j, c * cols:(c + 1) * cols, :])
        r0s[c] = (far + jnp.where(j == c, vbuf[half_o, :], 0.0)).astype(bf16)
    r0_copy = remote(r0s, r0r, xsend.at[slot], xrecv.at[slot], partner)
    r0_copy.start()
    pending.append(r0_copy)
    slot_r0 = slot

    s_copies = []
    for d in peers:
        block = pl.ds(pl.multiple_of(to_peer[d - 1] * blk, blk), blk)
        s_copies.append(
            remote(states.at[:, :, block], stg.at[:, own_rows, :], ssend.at[d - 1],
                   srecv.at[d - 1], {"dp": to_peer[d - 1]})
        )
        s_copies[-1].start()

    s_near = sbuf[half_j, :]
    for c in range(2):
        near = step_size * back_product(s_near, cw[j, c * cols:(c + 1) * cols, :])
        near = near + jnp.where(j == c, vbuf[half_j, :], 0.0)
        resid[c] = near - guess[0, half_j, c * cols:(c + 1) * cols].astype(f32)
    for c_copy in c_copies:
        c_copy.wait_recv()
    cslopes[j] = slopes[0, half_j, :]
    cslopes[o] = slope_of(states[0, half_j, :], cw[o])
    r0_copy.wait_recv()
    for c in range(2):
        resid[c] = resid[c] + r0r[c].astype(f32)

    for layer in range(layers):
        stg[layer, own_rows, :] = states[layer, :, own_in]
    for s_copy in s_copies:
        s_copy.wait_recv()
    for layer in range(layers):
        stt[layer] = stg[layer].T

    chain = [
        remote(ebuf.at[c], inc.at[c], hsend.at[c], hrecv.at[c], {"layer": slab - 1})
        for c in range(2)
    ]

    @pl.when(not_top)
    def _():
        for c in range(2):
            chain[c].wait_recv()

    @pl.when(jnp.logical_not(not_top))
    def _():
        inc[...] = jnp.zeros_like(inc)

    pass_on = remote(inc.at[o], oinc, xsend.at[slot + 1], xrecv.at[slot + 1], partner)
    pass_on.start()
    pending.append(pass_on)
    carried = [inc[c].astype(f32) for c in range(2)]
    coarse_scaled = [(carried[c] * cslopes[c]).astype(bf16) for c in range(2)]
    for c in range(2):
        block = slice(c * cols, (c + 1) * cols)
        product = back_product(coarse_scaled[0], cw[0, block, :]) + back_product(
            coarse_scaled[1], cw[1, block, :]
        )
        ebuf[c] = (carried[c] + layers * step_size * product + resid[c]).astype(bf16)

        @pl.when(not_low)
        def _():
            chain[c].start()

    e_copy = remote(ebuf.at[o], oe, xsend.at[slot + 2], xrecv.at[slot + 2], partner)
    e_copy.start()
    pending.append(e_copy)

    vbuf[half_j, :] = terminal[half_j, :] + inc[j].astype(f32)
    pass_on.wait_recv()
    vbuf[half_o, :] = terminal[half_o, :] + oinc[...].astype(f32)
    v = vbuf[...]
    g_copies = {}

    def spread(layer, s):
        sg[layer, own_rows, :] = s
        for d in peers:
            g_copies[layer, d] = remote(
                sg.at[layer, own_rows], sg.at[layer, own_rows],
                gsend.at[layer, d - 1], grecv.at[layer, d - 1], {"dp": to_peer[d - 1]},
            )
            g_copies[layer, d].start()

    def gradient(layer):
        for d in peers:
            g_copies[layer, d].wait_recv()
        grads[layer] = step_size * jnp.dot(stt[layer], sg[layer], preferred_element_type=f32)

    slot = slot_r0 + 3
    for layer in range(layers - 1, 0, -1):
        s = (v * slopes[layer]).astype(bf16)
        spread(layer, s)
        between = functools.partial(gradient, layer + 1) if layer < layers - 1 else None
        v = exchange_step(slot, layer, v, s, between)
        slot += 1
        adjoint[layer] = v.astype(bf16)
    spread(0, (v * slopes[0]).astype(bf16))
    if layers > 1:
        gradient(1)
    e_copy.wait_recv()
    adjoint[0, half_j, :] = (guess[0, half_j, cols_j].astype(f32) + ebuf[j].astype(f32)).astype(bf16)
    adjoint[0, half_o, :] = (guess[0, half_o, cols_j].astype(f32) + oe[...].astype(f32)).astype(bf16)
    gradient(0)

    for copy in pending + c_copies + s_copies + list(w_copies.values()) + list(g_copies.values()):
        copy.wait_send()

    @pl.when(not_low)
    def _():
        point_copy.wait_send()
        for c in range(2):
            chain[c].wait_send()


def solution(mesh):
    slab_count, dp_count, mp_count = (mesh.shape[a] for a in ("layer", "dp", "mp"))
    assert mp_count == 2

    def body(states, weights, guess_points, cotangent):
        layers, rows, width = states.shape
        blk, cols = weights.shape[1:]
        assert guess_points.shape[0] == 1
        half = rows // 2
        slots = 2 * layers + 2
        all_rows = rows * dp_count
        dma = pltpu.SemaphoreType.DMA
        vmem = pl.BlockSpec(memory_space=pltpu.VMEM)
        return pl.pallas_call(
            functools.partial(cycle, slab_count, dp_count, layers),
            out_shape=(
                jax.ShapeDtypeStruct((layers, rows, cols), bf16),
                jax.ShapeDtypeStruct((layers, blk, cols), f32),
            ),
            in_specs=[vmem] * 4,
            out_specs=(vmem, vmem),
            scratch_shapes=[
                pltpu.VMEM((layers - 1, width, cols), bf16),
                pltpu.VMEM((2, width, cols), bf16),
                pltpu.VMEM((rows, cols), bf16),
                pltpu.VMEM((layers, rows, cols), f32),
                pltpu.VMEM((2, half, cols), f32),
                pltpu.VMEM((rows, cols), f32),
                pltpu.VMEM((rows, cols), bf16),
                pltpu.VMEM((rows, cols), f32),
                pltpu.VMEM((slots, rows, cols), bf16),
                pltpu.VMEM((slots, rows, cols), bf16),
                pltpu.VMEM((2, half, cols), bf16),
                pltpu.VMEM((2, half, cols), bf16),
                pltpu.VMEM((2, half, cols), f32),
                pltpu.VMEM((2, half, cols), bf16),
                pltpu.VMEM((half, cols), bf16),
                pltpu.VMEM((2, half, cols), bf16),
                pltpu.VMEM((half, cols), bf16),
                pltpu.VMEM((layers, all_rows, cols), bf16),
                pltpu.VMEM((layers, all_rows, blk), bf16),
                pltpu.VMEM((layers, blk, all_rows), bf16),
                dma((layers, dp_count - 1)), dma((layers, dp_count - 1)),
                dma((dp_count,)), dma((dp_count,)),
                dma((layers,)),
                dma((dp_count - 1,)), dma((dp_count - 1,)),
                dma((layers, dp_count - 1)), dma((layers, dp_count - 1)),
                dma((slots,)), dma((slots,)),
                dma((1,)), dma((1,)),
                dma((2,)), dma((2,)),
            ],
            compiler_params=pltpu.CompilerParams(
                collective_id=0, has_side_effects=True, vmem_limit_bytes=56 * 2**20
            ),
            cost_estimate=pl.CostEstimate(
                flops=12 * layers * rows * width * cols, bytes_accessed=2**23, transcendentals=0
            ),
        )(states, weights, guess_points, cotangent)

    return jax.shard_map(
        body,
        mesh=mesh,
        in_specs=(
            P("layer", "dp", None),
            P("layer", "dp", "mp"),
            P("layer", "dp", None),
            P("dp", None),
        ),
        out_specs=(P("layer", "dp", "mp"), P("layer", "dp", "mp")),
        check_vma=False,
    )
```

time: 467 us -> 121 us (0.26)
  waiting for transfers between devices: 373 us -> 0 us
  Pallas kernels: 0 us -> 114 us
  matrix products: 31.6 us -> 0 us
  other arithmetic: 17.4 us -> 0 us
  between operations: 14.4 us -> 0.64 us
  starting transfers between devices: 10.7 us -> 0 us
  blocking collectives: 9.56 us -> 0 us
    psum x7 -> x0, waiting for transfers between devices: 191 us -> none  [fine_step(): summed = lax.psum(back_product(scaled_rows, gathered[layer_id]), 'mp')]
    pallas_call x0 -> x1, Pallas kernels: none -> 114 us  [body(): pl.pallas_call(functools.partial(cycle, slab_count, dp_count, layers), ou...]
    all_gather x2 -> x0, waiting for transfers between devices: 90.6 us -> none  [the longest x1 56.4 us: body(): gathered = lax.all_gather(weights, 'dp', axis=1, tiled=True)]
    reduce_scatter x1 -> x0, waiting for transfers between devices: 52.7 us -> none  [body(): lax.psum_scatter(partial_terms.astype(jnp.bfloat16), 'dp', scatter_dimens...]
    ppermute x8 -> x0, waiting for transfers between devices: 38.5 us -> none  [from_behind(): lax.ppermute(value, axis, [(source, source + steps) for source in range(l...]
    dot_general x14 -> x0, matrix products: 31.6 us -> none  [the longest x8 19.9 us: back_product(): lax.dot_general(scaled_rows, weight_block, (((1,), (1,)), ((), ())), pref...]
    ppermute x8 -> x0, starting transfers between devices: 10.3 us -> none  [from_behind(): lax.ppermute(value, axis, [(source, source + steps) for source in range(l...]
    all_gather x1 -> x0, blocking collectives: 9.56 us -> none  [body(): lax.all_gather(shortened(jnp.concatenate([errors, incoming[None]], 0)), '...]
  transfers between devices with their start and end apart: 18 -> 0, of which waited for: 18 -> 0; matrix products, arithmetic and copies ran while one was open for 2% -> 0% of each run, Pallas kernels for 0% -> 0%
where the time goes in v1:
time: 121 us
  Pallas kernels  114 us (94%)
  local copies, waits for them, and re-layouts  6.51 us (5%)
    pallas_call x1, Pallas kernels, body(): pl.pallas_call(functools.partial(cycle, slab_count, dp_count, layers), ou...  114 us
    unnamed x2, local copies, waits for them, and re-layouts  6.51 us

profile of v1, /device:TPU:0, one launch (start us, length us, event | category | flops | bytes accessed | tf_op | source)
XLA Modules:
  0.0 121.2 jit_solution(621343116421640019)
XLA Ops:
  0.6 114.1 %shard_map.59 = (bf16[4,128,512]{2,1,0:T(8,128)(2,1)}, f32[4,512,512]{2,1,0:T(8,128)}) custom-call(bf16[4,128,1024]{2,1,0:T(8,128)(2,1)} %states.1, bf16[4,512,512]{2,1,0:T(8,128)(2,1)} %weights.1, bf16[1,128,1024]{2,1,0:T(8,128)(2,1)} %guess.1, bf16[128,1024]{1,0:T(8,128)(2,1)} %cotangent.1), custom_call_target="tpu_custom_call" | custom-call | flops 3221225472 | bytes 8388608 | tf_op jit(solution)/shard_map/pallas_call | solution.py:280
  114.7 1.9 %copy.8 = bf16[4,128,512]{2,1,0:T(8,128)(2,1)} copy(bf16[4,128,512]{2,1,0:T(8,128)(2,1)} %get-tuple-element.4) | data formatting | bytes 1048576
  116.6 4.6 %copy.9 = f32[4,512,512]{2,1,0:T(8,128)} copy(f32[4,512,512]{2,1,0:T(8,128)} %get-tuple-element.5) | data formatting | bytes 8388608

commit v2 on v1

--- a/solution.py
+++ b/solution.py
@@ -25,10 +25,10 @@
 
 def cycle(
     slab_count, dp_count, layers,
-    states, weights, guess, cotangent, adjoint, grads,
-    gw, cw, npt, slopes, cslopes, vbuf, sbuf, terminal,
-    exs, exr, r0s, r0r, resid, inc, oinc, ebuf, oe, sg, stg, stt,
-    wsend, wrecv, csend, crecv, lsem, ssend, srecv, gsend, grecv,
+    states_in, weights, guess, cotangent, adjoint, sg, stg,
+    states, gw, cw, npt, slopes, cslopes, vbuf, sbuf, terminal,
+    exs, exr, r0s, r0r, resid, inc, oinc, ebuf, oe, sown,
+    wsend, wrecv, csend, crecv, lsem, osem, ssend, srecv, gsend, grecv,
     xsend, xrecv, nsend, nrecv, hsend, hrecv,
 ):
     slab, mine, j = lax.axis_index("layer"), lax.axis_index("dp"), lax.axis_index("mp")
@@ -74,6 +74,9 @@
         barrier, dp_count + not_top.astype(jnp.int32) + not_low.astype(jnp.int32)
     )
 
+    states_copy = pltpu.make_async_copy(states_in, states, osem.at[0])
+    states_copy.start()
+
     def home(layer):
         return cw.at[j] if layer == 0 else gw.at[layer - 1]
 
@@ -118,19 +121,18 @@
             remote(cw.at[j, block], cw.at[j, block], csend.at[d], crecv.at[d], partner)
         )
         c_copies[d].start()
+    states_copy.wait()
     slopes[0] = slope_of(states[0], cw[j])
 
     pending = []
 
-    def exchange_step(slot, layer, v, s, between=None):
+    def exchange_step(slot, layer, v, s):
         w = home(layer)
         exs[slot] = (step_size * back_product(s, w[cols_o, :])).astype(bf16)
         copy = remote(exs.at[slot], exr.at[slot], xsend.at[slot], xrecv.at[slot], partner)
         copy.start()
         pending.append(copy)
         v = v + step_size * back_product(s, w[cols_j, :])
-        if between is not None:
-            between()
         copy.wait_recv()
         return v + exr[slot].astype(f32)
 
@@ -159,10 +161,15 @@
     for d in peers:
         block = pl.ds(pl.multiple_of(to_peer[d - 1] * blk, blk), blk)
         s_copies.append(
-            remote(states.at[:, :, block], stg.at[:, own_rows, :], ssend.at[d - 1],
+            remote(states_in.at[:, :, block], stg.at[:, own_rows, :], ssend.at[d - 1],
                    srecv.at[d - 1], {"dp": to_peer[d - 1]})
         )
         s_copies[-1].start()
+
+    own_states = pltpu.make_async_copy(
+        states_in.at[:, :, own_in], stg.at[:, own_rows, :], osem.at[1]
+    )
+    own_states.start()
 
     s_near = sbuf[half_j, :]
     for c in range(2):
@@ -177,42 +184,41 @@
     for c in range(2):
         resid[c] = resid[c] + r0r[c].astype(f32)
 
-    for layer in range(layers):
-        stg[layer, own_rows, :] = states[layer, :, own_in]
-    for s_copy in s_copies:
-        s_copy.wait_recv()
-    for layer in range(layers):
-        stt[layer] = stg[layer].T
-
     chain = [
         remote(ebuf.at[c], inc.at[c], hsend.at[c], hrecv.at[c], {"layer": slab - 1})
         for c in range(2)
     ]
 
-    @pl.when(not_top)
-    def _():
-        for c in range(2):
+    @pl.when(jnp.logical_not(not_top))
+    def _():
+        inc[...] = jnp.zeros_like(inc)
+
+    carried, products = [], [0.0, 0.0]
+    blocks = [slice(n * cols, (n + 1) * cols) for n in range(2)]
+
+    def chain_out(n):
+        total = carried[n] + layers * step_size * products[n] + resid[n]
+        ebuf[n] = total.astype(bf16)
+
+        @pl.when(not_low)
+        def _():
+            chain[n].start()
+
+    for c in range(2):
+
+        @pl.when(not_top)
+        def _():
             chain[c].wait_recv()
 
-    @pl.when(jnp.logical_not(not_top))
-    def _():
-        inc[...] = jnp.zeros_like(inc)
-
+        carried.append(inc[c].astype(f32))
+        scaled_rows = (carried[c] * cslopes[c]).astype(bf16)
+        for n in range(2):
+            products[n] = products[n] + back_product(scaled_rows, cw[c, blocks[n], :])
+            if c == 1:
+                chain_out(n)
     pass_on = remote(inc.at[o], oinc, xsend.at[slot + 1], xrecv.at[slot + 1], partner)
     pass_on.start()
     pending.append(pass_on)
-    carried = [inc[c].astype(f32) for c in range(2)]
-    coarse_scaled = [(carried[c] * cslopes[c]).astype(bf16) for c in range(2)]
-    for c in range(2):
-        block = slice(c * cols, (c + 1) * cols)
-        product = back_product(coarse_scaled[0], cw[0, block, :]) + back_product(
-            coarse_scaled[1], cw[1, block, :]
-        )
-        ebuf[c] = (carried[c] + layers * step_size * product + resid[c]).astype(bf16)
-
-        @pl.when(not_low)
-        def _():
-            chain[c].start()
 
     e_copy = remote(ebuf.at[o], oe, xsend.at[slot + 2], xrecv.at[slot + 2], partner)
     e_copy.start()
@@ -224,36 +230,36 @@
     v = vbuf[...]
     g_copies = {}
 
+    own_scaled = []
+
     def spread(layer, s):
-        sg[layer, own_rows, :] = s
+        sown[layer] = s
         for d in peers:
             g_copies[layer, d] = remote(
-                sg.at[layer, own_rows], sg.at[layer, own_rows],
+                sown.at[layer], sg.at[layer, own_rows],
                 gsend.at[layer, d - 1], grecv.at[layer, d - 1], {"dp": to_peer[d - 1]},
             )
             g_copies[layer, d].start()
-
-    def gradient(layer):
-        for d in peers:
-            g_copies[layer, d].wait_recv()
-        grads[layer] = step_size * jnp.dot(stt[layer], sg[layer], preferred_element_type=f32)
+        own_scaled.append(
+            pltpu.make_async_copy(sown.at[layer], sg.at[layer, own_rows], osem.at[2 + layer])
+        )
+        own_scaled[-1].start()
 
     slot = slot_r0 + 3
     for layer in range(layers - 1, 0, -1):
         s = (v * slopes[layer]).astype(bf16)
         spread(layer, s)
-        between = functools.partial(gradient, layer + 1) if layer < layers - 1 else None
-        v = exchange_step(slot, layer, v, s, between)
+        v = exchange_step(slot, layer, v, s)
         slot += 1
         adjoint[layer] = v.astype(bf16)
     spread(0, (v * slopes[0]).astype(bf16))
-    if layers > 1:
-        gradient(1)
     e_copy.wait_recv()
     adjoint[0, half_j, :] = (guess[0, half_j, cols_j].astype(f32) + ebuf[j].astype(f32)).astype(bf16)
     adjoint[0, half_o, :] = (guess[0, half_o, cols_j].astype(f32) + oe[...].astype(f32)).astype(bf16)
-    gradient(0)
-
+    for copy in s_copies + list(g_copies.values()):
+        copy.wait_recv()
+    for copy in own_scaled + [own_states]:
+        copy.wait()
     for copy in pending + c_copies + s_copies + list(w_copies.values()) + list(g_copies.values()):
         copy.wait_send()
 
@@ -262,6 +268,14 @@
         point_copy.wait_send()
         for c in range(2):
             chain[c].wait_send()
+
+
+def weight_gradients(inputs, scaled, adjoint_in, grads, adjoint):
+    product = lax.dot_general(
+        inputs[0], scaled[0], (((0,), (0,)), ((), ())), preferred_element_type=f32
+    )
+    grads[0] = step_size * product
+    adjoint[...] = adjoint_in[...]
 
 
 def solution(mesh):
@@ -277,15 +291,18 @@
         all_rows = rows * dp_count
         dma = pltpu.SemaphoreType.DMA
         vmem = pl.BlockSpec(memory_space=pltpu.VMEM)
-        return pl.pallas_call(
+        anywhere = pl.BlockSpec(memory_space=pl.ANY)
+        adjoint, scaled, inputs = pl.pallas_call(
             functools.partial(cycle, slab_count, dp_count, layers),
             out_shape=(
                 jax.ShapeDtypeStruct((layers, rows, cols), bf16),
-                jax.ShapeDtypeStruct((layers, blk, cols), f32),
+                jax.ShapeDtypeStruct((layers, all_rows, cols), bf16),
+                jax.ShapeDtypeStruct((layers, all_rows, blk), bf16),
             ),
-            in_specs=[vmem] * 4,
-            out_specs=(vmem, vmem),
+            in_specs=[anywhere, anywhere, vmem, vmem],
+            out_specs=(vmem, anywhere, anywhere),
             scratch_shapes=[
+                pltpu.VMEM((layers, rows, width), bf16),
                 pltpu.VMEM((layers - 1, width, cols), bf16),
                 pltpu.VMEM((2, width, cols), bf16),
                 pltpu.VMEM((rows, cols), bf16),
@@ -303,12 +320,10 @@
                 pltpu.VMEM((half, cols), bf16),
                 pltpu.VMEM((2, half, cols), bf16),
                 pltpu.VMEM((half, cols), bf16),
-                pltpu.VMEM((layers, all_rows, cols), bf16),
-                pltpu.VMEM((layers, all_rows, blk), bf16),
-                pltpu.VMEM((layers, blk, all_rows), bf16),
+                pltpu.VMEM((layers, rows, cols), bf16),
                 dma((layers, dp_count - 1)), dma((layers, dp_count - 1)),
                 dma((dp_count,)), dma((dp_count,)),
-                dma((layers,)),
+                dma((layers,)), dma((layers + 2,)),
                 dma((dp_count - 1,)), dma((dp_count - 1,)),
                 dma((layers, dp_count - 1)), dma((layers, dp_count - 1)),
                 dma((slots,)), dma((slots,)),
@@ -323,6 +338,22 @@
             ),
         )(states, weights, guess_points, cotangent)
 
+        def per_layer(*shape):
+            return pl.BlockSpec((1, *shape), lambda layer: (layer, 0, 0))
+
+        grads, adjoint = pl.pallas_call(
+            weight_gradients,
+            grid=(layers,),
+            out_shape=(
+                jax.ShapeDtypeStruct((layers, blk, cols), f32),
+                jax.ShapeDtypeStruct((layers, rows, cols), bf16),
+            ),
+            in_specs=[per_layer(all_rows, blk), per_layer(all_rows, cols), per_layer(rows, cols)],
+            out_specs=(per_layer(blk, cols), per_layer(rows, cols)),
+            compiler_params=pltpu.CompilerParams(vmem_limit_bytes=32 * 2**20),
+        )(inputs, scaled, adjoint)
+        return adjoint, grads
+
     return jax.shard_map(
         body,
         mesh=mesh,

time: 121 us -> 111 us (0.917); the launches traced: 121 us -> 110 us
  Pallas kernels: 114 us -> 106 us
  local copies, waits for them, and re-layouts: 6.51 us -> 3.48 us
    pallas_call x1, Pallas kernels: 114 us -> 103 us  [body(): pl.pallas_call(functools.partial(cycle, slab_count, dp_count, layers), ou...]
    unnamed x2 -> x6, local copies, waits for them, and re-layouts: 6.51 us -> 3.48 us
    pallas_call x0 -> x1, Pallas kernels: none -> 2.98 us  [body(): pl.pallas_call(weight_gradients, grid=(layers,), out_shape=(jax.ShapeDtyp...]
where the time goes in v2:
time: 111 us; the launch traced here: 110 us
  Pallas kernels  106 us (95%)
  local copies, waits for them, and re-layouts  3.48 us (3%)
    pallas_call x1, Pallas kernels, body(): pl.pallas_call(functools.partial(cycle, slab_count, dp_count, layers), ou...  103 us
    unnamed x6, local copies, waits for them, and re-layouts  3.48 us
    pallas_call x1, Pallas kernels, body(): pl.pallas_call(weight_gradients, grid=(layers,), out_shape=(jax.ShapeDtyp...  2.98 us

profile of v2, /device:TPU:0, one launch (start us, length us, event | category | flops | bytes accessed | tf_op | source)
XLA Modules:
  0.0 109.9 jit_solution(9365674328913003585)
XLA Ops:
  0.6 102.8 %shard_map.59 = (bf16[4,128,512]{2,1,0:T(8,128)(2,1)}, bf16[4,256,512]{2,1,0:T(8,128)(2,1)}, bf16[4,256,512]{2,1,0:T(8,128)(2,1)}) custom-call(bf16[4,128,1024]{2,1,0:T(8,128)(2,1)} %states_in.1, bf16[4,512,512]{2,1,0:T(8,128)(2,1)} %weights.1, bf16[1,128,1024]{2,1,0:T(8,128)(2,1)} %guess.1, bf16[128,1024]{1,0:T(8,128)(2,1)} %cotangent.1), custom_call_target="tpu_custom_call" | custom-call | flops 3221225472 | bytes 8388608 | tf_op jit(solution)/shard_map/pallas_call | solution.py:295
  103.4 0.0 copy-start
  103.4 1.2 %copy-done = bf16[4,256,512]{2,1,0:T(8,128)(2,1)S(1)} copy-done((bf16[4,256,512]{2,1,0:T(8,128)(2,1)S(1)}, bf16[4,256,512]{2,1,0:T(8,128)(2,1)}, u32[]{:S(2)}) %copy-start) | copy-done | bytes 1048600
  104.6 0.0 copy-start.1
  104.6 1.2 %copy-done.1 = bf16[4,256,512]{2,1,0:T(8,128)(2,1)S(1)} copy-done((bf16[4,256,512]{2,1,0:T(8,128)(2,1)S(1)}, bf16[4,256,512]{2,1,0:T(8,128)(2,1)}, u32[]{:S(2)}) %copy-start.1) | copy-done | bytes 1048600
  105.9 0.0 copy-start.2
  105.9 1.0 copy-done.2
  106.9 3.0 %shard_map.60 = (f32[4,512,512]{2,1,0:T(8,128)}, bf16[4,128,512]{2,1,0:T(8,128)(2,1)}) custom-call(bf16[4,256,512]{2,1,0:T(8,128)(2,1)S(1)} %copy-done.1, bf16[4,256,512]{2,1,0:T(8,128)(2,1)S(1)} %copy-done, bf16[4,128,512]{2,1,0:T(8,128)(2,1)S(1)} %copy-done.2), custom_call_target="tpu_custom_call" | custom-call | tf_op jit(solution)/shard_map/pallas_call | solution.py:344
Async XLA Ops:
  103.4 1.2 %copy-start = (bf16[4,256,512]{2,1,0:T(8,128)(2,1)S(1)}, bf16[4,256,512]{2,1,0:T(8,128)(2,1)}, u32[]{:S(2)}) copy-start(bf16[4,256,512]{2,1,0:T(8,128)(2,1)} %get-tuple-element.8.scaled) | copy-start | bytes 3145732
  104.6 1.2 %copy-start.1 = (bf16[4,256,512]{2,1,0:T(8,128)(2,1)S(1)}, bf16[4,256,512]{2,1,0:T(8,128)(2,1)}, u32[]{:S(2)}) copy-start(bf16[4,256,512]{2,1,0:T(8,128)(2,1)} %get-tuple-element.7.inputs) | copy-start | bytes 3145732
  105.9 1.0 copy-start.2

commit v3 on v2

--- a/solution.py
+++ b/solution.py
@@ -29,7 +29,7 @@
     states, gw, cw, npt, slopes, cslopes, vbuf, sbuf, terminal,
     exs, exr, r0s, r0r, resid, inc, oinc, ebuf, oe, sown,
     wsend, wrecv, csend, crecv, lsem, osem, ssend, srecv, gsend, grecv,
-    xsend, xrecv, nsend, nrecv, hsend, hrecv,
+    xsend, xrecv, rsend, rrecv, psend, precv, nsend, nrecv, hsend, hrecv,
 ):
     slab, mine, j = lax.axis_index("layer"), lax.axis_index("dp"), lax.axis_index("mp")
     o = 1 - j
@@ -88,16 +88,27 @@
         point_copy.start()
 
     w_copies, local_copies = {}, {}
-    c_copies = [remote(weights.at[0], cw.at[j, own_in], csend.at[0], crecv.at[0], partner)]
+    pieces = 4
+    piece = blk // pieces
+
+    def piece_of(owner, n):
+        return pl.ds(pl.multiple_of(owner * blk + n * piece, piece), piece)
+
+    c_copies = [remote(weights.at[0], cw.at[j, own_in], csend.at[0, 0], crecv.at[0, 0], partner)]
     c_copies[0].start()
-    order = [0] + list(range(layers - 1, 0, -1))
+    order = range(layers - 1, -1, -1)
     for layer in order:
-        for d in peers:
-            w_copies[layer, d] = remote(
-                weights.at[layer], home(layer).at[own_in],
-                wsend.at[layer, d - 1], wrecv.at[layer, d - 1], {"dp": to_peer[d - 1]},
-            )
-            w_copies[layer, d].start()
+        parts = pieces if layer == 0 else 1
+        for n in range(parts):
+            for d in peers:
+                source = weights.at[layer, n * piece:(n + 1) * piece] if layer == 0 else weights.at[layer]
+                target = cw.at[j, piece_of(mine, n)] if layer == 0 else home(layer).at[own_in]
+                sem = pieces - 1 + layer if layer else n
+                w_copies[layer, n, d] = remote(
+                    source, target, wsend.at[sem, d - 1], wrecv.at[sem, d - 1],
+                    {"dp": to_peer[d - 1]},
+                )
+                w_copies[layer, n, d].start()
     for layer in order:
         local_copies[layer] = pltpu.make_async_copy(
             weights.at[layer], home(layer).at[own_in], lsem.at[layer]
@@ -113,49 +124,58 @@
     def _():
         terminal[...] = cotangent[:, cols_j].astype(f32)
 
-    local_copies[0].wait()
-    for d in peers:
-        w_copies[0, d].wait_recv()
-        block = pl.ds(pl.multiple_of(from_peer[d - 1] * blk, blk), blk)
-        c_copies.append(
-            remote(cw.at[j, block], cw.at[j, block], csend.at[d], crecv.at[d], partner)
-        )
-        c_copies[d].start()
-    states_copy.wait()
-    slopes[0] = slope_of(states[0], cw[j])
-
     pending = []
-
-    def exchange_step(slot, layer, v, s):
+    span = [slice(0, half), slice(half, 2 * half)]
+
+    def fine_half(slot, h, layer, scaled_rows):
         w = home(layer)
-        exs[slot] = (step_size * back_product(s, w[cols_o, :])).astype(bf16)
-        copy = remote(exs.at[slot], exr.at[slot], xsend.at[slot], xrecv.at[slot], partner)
+        exs[slot, h] = (step_size * back_product(scaled_rows, w[cols_o, :])).astype(bf16)
+        copy = remote(
+            exs.at[slot, h], exr.at[slot, h], xsend.at[slot, h], xrecv.at[slot, h], partner
+        )
         copy.start()
         pending.append(copy)
-        v = v + step_size * back_product(s, w[cols_j, :])
+        return copy, step_size * back_product(scaled_rows, w[cols_j, :])
+
+    def arrived(value, copy, slot, h):
+        if copy is None:
+            return value
         copy.wait_recv()
-        return v + exr[slot].astype(f32)
-
-    v = terminal[...]
-    slot = 0
-    for layer in range(layers - 1, 0, -1):
+        return value + exr[slot, h].astype(f32)
+
+    v = [terminal[span[h], :] for h in range(2)]
+    flying = [None, None]
+    states_copy.wait()
+    for slot, layer in enumerate(range(layers - 1, 0, -1)):
         local_copies[layer].wait()
         for d in peers:
-            w_copies[layer, d].wait_recv()
+            w_copies[layer, 0, d].wait_recv()
         slopes[layer] = slope_of(states[layer], gw[layer - 1])
-        s = (v * slopes[layer]).astype(bf16)
-        v = exchange_step(slot, layer, v, s)
-        slot += 1
-    vbuf[...] = v
-    sbuf[...] = (v * slopes[0]).astype(bf16)
+        for h in range(2):
+            v[h] = arrived(v[h], flying[h], slot - 1, h)
+            scaled_rows = (v[h] * slopes[layer, span[h], :]).astype(bf16)
+            flying[h], term = fine_half(slot, h, layer, scaled_rows)
+            v[h] = v[h] + term
+    local_copies[0].wait()
+    for n in range(pieces):
+        for d in peers:
+            w_copies[0, n, d].wait_recv()
+            block = cw.at[j, piece_of(from_peer[d - 1], n)]
+            c_copies.append(remote(block, block, csend.at[d, n], crecv.at[d, n], partner))
+            c_copies[-1].start()
+    slopes[0] = slope_of(states[0], cw[j])
+    for h in range(2):
+        v[h] = arrived(v[h], flying[h], layers - 2, h)
+        vbuf[span[h], :] = v[h]
+        sbuf[span[h], :] = (v[h] * slopes[0, span[h], :]).astype(bf16)
+    r0_copies = []
     s_far = sbuf[half_o, :]
     for c in range(2):
         far = step_size * back_product(s_far, cw[j, c * cols:(c + 1) * cols, :])
         r0s[c] = (far + jnp.where(j == c, vbuf[half_o, :], 0.0)).astype(bf16)
-    r0_copy = remote(r0s, r0r, xsend.at[slot], xrecv.at[slot], partner)
-    r0_copy.start()
-    pending.append(r0_copy)
-    slot_r0 = slot
+        r0_copies.append(remote(r0s.at[c], r0r.at[c], rsend.at[c], rrecv.at[c], partner))
+        r0_copies[c].start()
+    pending += r0_copies
 
     s_copies = []
     for d in peers:
@@ -176,64 +196,66 @@
         near = step_size * back_product(s_near, cw[j, c * cols:(c + 1) * cols, :])
         near = near + jnp.where(j == c, vbuf[half_j, :], 0.0)
         resid[c] = near - guess[0, half_j, c * cols:(c + 1) * cols].astype(f32)
+    chain = [
+        remote(ebuf.at[c], inc.at[c], hsend.at[c], hrecv.at[c], {"layer": slab - 1})
+        for c in range(2)
+    ]
+
+    pass_on = remote(inc.at[o], oinc, psend.at[0], precv.at[0], partner)
+
+    @pl.when(jnp.logical_not(not_top))
+    def _():
+        inc[...] = jnp.zeros_like(inc)
+        pass_on.start()
+
+    for c in range(2):
+        r0_copies[c].wait_recv()
+        resid[c] = resid[c] + r0r[c].astype(f32)
+
+        @pl.when(jnp.logical_not(not_top))
+        def _():
+            ebuf[c] = resid[c].astype(bf16)
+            chain[c].start()
+
     for c_copy in c_copies:
         c_copy.wait_recv()
     cslopes[j] = slopes[0, half_j, :]
     cslopes[o] = slope_of(states[0, half_j, :], cw[o])
-    r0_copy.wait_recv()
-    for c in range(2):
-        resid[c] = resid[c] + r0r[c].astype(f32)
-
-    chain = [
-        remote(ebuf.at[c], inc.at[c], hsend.at[c], hrecv.at[c], {"layer": slab - 1})
-        for c in range(2)
-    ]
-
-    @pl.when(jnp.logical_not(not_top))
-    def _():
-        inc[...] = jnp.zeros_like(inc)
-
-    carried, products = [], [0.0, 0.0]
-    blocks = [slice(n * cols, (n + 1) * cols) for n in range(2)]
-
-    def chain_out(n):
-        total = carried[n] + layers * step_size * products[n] + resid[n]
-        ebuf[n] = total.astype(bf16)
-
-        @pl.when(not_low)
-        def _():
-            chain[n].start()
-
-    for c in range(2):
-
-        @pl.when(not_top)
-        def _():
+
+    @pl.when(not_top)
+    def _():
+        carried, products = [], [0.0, 0.0]
+        for c in range(2):
             chain[c].wait_recv()
-
-        carried.append(inc[c].astype(f32))
-        scaled_rows = (carried[c] * cslopes[c]).astype(bf16)
-        for n in range(2):
-            products[n] = products[n] + back_product(scaled_rows, cw[c, blocks[n], :])
             if c == 1:
-                chain_out(n)
-    pass_on = remote(inc.at[o], oinc, xsend.at[slot + 1], xrecv.at[slot + 1], partner)
-    pass_on.start()
-    pending.append(pass_on)
-
-    e_copy = remote(ebuf.at[o], oe, xsend.at[slot + 2], xrecv.at[slot + 2], partner)
+                pass_on.start()
+            carried.append(inc[c].astype(f32))
+            scaled_rows = (carried[c] * cslopes[c]).astype(bf16)
+            for n in range(2):
+                block = cw[c, n * cols:(n + 1) * cols, :]
+                products[n] = products[n] + back_product(scaled_rows, block)
+                if c == 1:
+                    total = carried[n] + layers * step_size * products[n] + resid[n]
+                    ebuf[n] = total.astype(bf16)
+
+                    @pl.when(not_low)
+                    def _():
+                        chain[n].start()
+
+    e_copy = remote(ebuf.at[o], oe, psend.at[1], precv.at[1], partner)
     e_copy.start()
-    pending.append(e_copy)
+    pending += [pass_on, e_copy]
 
     vbuf[half_j, :] = terminal[half_j, :] + inc[j].astype(f32)
     pass_on.wait_recv()
     vbuf[half_o, :] = terminal[half_o, :] + oinc[...].astype(f32)
-    v = vbuf[...]
+    v = [vbuf[span[h], :] for h in range(2)]
+    flying = [None, None]
     g_copies = {}
 
     own_scaled = []
 
-    def spread(layer, s):
-        sown[layer] = s
+    def spread(layer):
         for d in peers:
             g_copies[layer, d] = remote(
                 sown.at[layer], sg.at[layer, own_rows],
@@ -245,14 +267,18 @@
         )
         own_scaled[-1].start()
 
-    slot = slot_r0 + 3
-    for layer in range(layers - 1, 0, -1):
-        s = (v * slopes[layer]).astype(bf16)
-        spread(layer, s)
-        v = exchange_step(slot, layer, v, s)
-        slot += 1
-        adjoint[layer] = v.astype(bf16)
-    spread(0, (v * slopes[0]).astype(bf16))
+    for layer in range(layers - 1, -1, -1):
+        slot = layers - 1 + (layers - 1 - layer)
+        for h in range(2):
+            v[h] = arrived(v[h], flying[h], slot - 1, h)
+            scaled_rows = (v[h] * slopes[layer, span[h], :]).astype(bf16)
+            sown[layer, span[h], :] = scaled_rows
+            if layer < layers - 1:
+                adjoint[layer + 1, span[h], :] = v[h].astype(bf16)
+            if layer:
+                flying[h], term = fine_half(slot, h, layer, scaled_rows)
+                v[h] = v[h] + term
+        spread(layer)
     e_copy.wait_recv()
     adjoint[0, half_j, :] = (guess[0, half_j, cols_j].astype(f32) + ebuf[j].astype(f32)).astype(bf16)
     adjoint[0, half_o, :] = (guess[0, half_o, cols_j].astype(f32) + oe[...].astype(f32)).astype(bf16)
@@ -287,7 +313,8 @@
         blk, cols = weights.shape[1:]
         assert guess_points.shape[0] == 1
         half = rows // 2
-        slots = 2 * layers + 2
+        slots = 2 * (layers - 1)
+        assert slab_count > 1 and layers > 1 and blk % 64 == 0
         all_rows = rows * dp_count
         dma = pltpu.SemaphoreType.DMA
         vmem = pl.BlockSpec(memory_space=pltpu.VMEM)
@@ -311,8 +338,8 @@
                 pltpu.VMEM((rows, cols), f32),
                 pltpu.VMEM((rows, cols), bf16),
                 pltpu.VMEM((rows, cols), f32),
-                pltpu.VMEM((slots, rows, cols), bf16),
-                pltpu.VMEM((slots, rows, cols), bf16),
+                pltpu.VMEM((slots, 2, half, cols), bf16),
+                pltpu.VMEM((slots, 2, half, cols), bf16),
                 pltpu.VMEM((2, half, cols), bf16),
                 pltpu.VMEM((2, half, cols), bf16),
                 pltpu.VMEM((2, half, cols), f32),
@@ -321,12 +348,14 @@
                 pltpu.VMEM((2, half, cols), bf16),
                 pltpu.VMEM((half, cols), bf16),
                 pltpu.VMEM((layers, rows, cols), bf16),
-                dma((layers, dp_count - 1)), dma((layers, dp_count - 1)),
-                dma((dp_count,)), dma((dp_count,)),
+                dma((layers + 3, dp_count - 1)), dma((layers + 3, dp_count - 1)),
+                dma((dp_count, 4)), dma((dp_count, 4)),
                 dma((layers,)), dma((layers + 2,)),
                 dma((dp_count - 1,)), dma((dp_count - 1,)),
                 dma((layers, dp_count - 1)), dma((layers, dp_count - 1)),
-                dma((slots,)), dma((slots,)),
+                dma((slots, 2)), dma((slots, 2)),
+                dma((2,)), dma((2,)),
+                dma((2,)), dma((2,)),
                 dma((1,)), dma((1,)),
                 dma((2,)), dma((2,)),
             ],
@@ -350,7 +379,7 @@
             ),
             in_specs=[per_layer(all_rows, blk), per_layer(all_rows, cols), per_layer(rows, cols)],
             out_specs=(per_layer(blk, cols), per_layer(rows, cols)),
-            compiler_params=pltpu.CompilerParams(vmem_limit_bytes=32 * 2**20),
+            compiler_params=pltpu.CompilerParams(vmem_limit_bytes=60 * 2**20),
         )(inputs, scaled, adjoint)
         return adjoint, grads
 

time: 111 us -> 108 us (0.973)
  local copies, waits for them, and re-layouts: 3.48 us -> 0 us
    unnamed x6 -> x0, local copies, waits for them, and re-layouts: 3.48 us -> none
    pallas_call x1, Pallas kernels: 2.98 us -> 4.8 us  [body(): pl.pallas_call(weight_gradients, grid=(layers,), out_shape=(jax.ShapeDtyp...]
where the time goes in v3:
time: 108 us; the launch traced here: 107 us
  Pallas kernels  107 us (99%)
    pallas_call x1, Pallas kernels, body(): pl.pallas_call(functools.partial(cycle, slab_count, dp_count, layers), ou...  102 us
    pallas_call x1, Pallas kernels, body(): pl.pallas_call(weight_gradients, grid=(layers,), out_shape=(jax.ShapeDtyp...  4.8 us

profile of v3, /device:TPU:0, one launch (start us, length us, event | category | flops | bytes accessed | tf_op | source)
XLA Modules:
  0.0 107.4 jit_solution(17905237427739820847)
XLA Ops:
  0.6 102.0 %shard_map.59 = (bf16[4,128,512]{2,1,0:T(8,128)(2,1)}, bf16[4,256,512]{2,1,0:T(8,128)(2,1)}, bf16[4,256,512]{2,1,0:T(8,128)(2,1)}) custom-call(bf16[4,128,1024]{2,1,0:T(8,128)(2,1)} %states_in.1, bf16[4,512,512]{2,1,0:T(8,128)(2,1)} %weights.1, bf16[1,128,1024]{2,1,0:T(8,128)(2,1)} %guess.1, bf16[128,1024]{1,0:T(8,128)(2,1)} %cotangent.1), custom_call_target="tpu_custom_call" | custom-call | flops 3221225472 | bytes 8388608 | tf_op jit(solution)/shard_map/pallas_call | solution.py:322
  102.6 4.8 %shard_map.60 = (f32[4,512,512]{2,1,0:T(8,128)}, bf16[4,128,512]{2,1,0:T(8,128)(2,1)}) custom-call(bf16[4,256,512]{2,1,0:T(8,128)(2,1)} %get-tuple-element.7.inputs, bf16[4,256,512]{2,1,0:T(8,128)(2,1)} %get-tuple-element.8.scaled, bf16[4,128,512]{2,1,0:T(8,128)(2,1)} %get-tuple-element.9.adjoint_in), custom_call_target="tpu_custom_call" | custom-call | tf_op jit(solution)/shard_map/pallas_call | solution.py:373

commit v4 on v3

--- a/solution.py
+++ b/solution.py
@@ -12,10 +12,8 @@
 MESH = pl.DeviceIdType.MESH
 
 
-def back_product(scaled_rows, weight_block):
-    return lax.dot_general(
-        scaled_rows, weight_block, (((1,), (1,)), ((), ())), preferred_element_type=f32
-    )
+def back_product(scaled_rows, turned_block):
+    return jnp.dot(scaled_rows, turned_block, preferred_element_type=f32)
 
 
 def slope_of(inputs, weight_block):
@@ -26,7 +24,7 @@
 def cycle(
     slab_count, dp_count, layers,
     states_in, weights, guess, cotangent, adjoint, sg, stg,
-    states, gw, cw, npt, slopes, cslopes, vbuf, sbuf, terminal,
+    states, gw, cw, wt, cwt, npt, slopes, cslopes, vbuf, sbuf, terminal,
     exs, exr, r0s, r0r, resid, inc, oinc, ebuf, oe, sown,
     wsend, wrecv, csend, crecv, lsem, osem, ssend, srecv, gsend, grecv,
     xsend, xrecv, rsend, rrecv, psend, precv, nsend, nrecv, hsend, hrecv,
@@ -128,14 +126,14 @@
     span = [slice(0, half), slice(half, 2 * half)]
 
     def fine_half(slot, h, layer, scaled_rows):
-        w = home(layer)
-        exs[slot, h] = (step_size * back_product(scaled_rows, w[cols_o, :])).astype(bf16)
+        w = wt.at[layer - 1]
+        exs[slot, h] = (step_size * back_product(scaled_rows, w[:, cols_o])).astype(bf16)
         copy = remote(
             exs.at[slot, h], exr.at[slot, h], xsend.at[slot, h], xrecv.at[slot, h], partner
         )
         copy.start()
         pending.append(copy)
-        return copy, step_size * back_product(scaled_rows, w[cols_j, :])
+        return copy, step_size * back_product(scaled_rows, w[:, cols_j])
 
     def arrived(value, copy, slot, h):
         if copy is None:
@@ -150,6 +148,7 @@
         local_copies[layer].wait()
         for d in peers:
             w_copies[layer, 0, d].wait_recv()
+        wt[layer - 1] = gw[layer - 1].T
         slopes[layer] = slope_of(states[layer], gw[layer - 1])
         for h in range(2):
             v[h] = arrived(v[h], flying[h], slot - 1, h)
@@ -157,12 +156,18 @@
             flying[h], term = fine_half(slot, h, layer, scaled_rows)
             v[h] = v[h] + term
     local_copies[0].wait()
+    cwt[j, :, own_in] = cw[j, own_in, :].T
     for n in range(pieces):
         for d in peers:
             w_copies[0, n, d].wait_recv()
             block = cw.at[j, piece_of(from_peer[d - 1], n)]
             c_copies.append(remote(block, block, csend.at[d, n], crecv.at[d, n], partner))
             c_copies[-1].start()
+            if piece % 128 == 0:
+                landed = piece_of(from_peer[d - 1], n)
+                cwt[j, :, landed] = cw[j, landed, :].T
+    if piece % 128:
+        cwt[j] = cw[j].T
     slopes[0] = slope_of(states[0], cw[j])
     for h in range(2):
         v[h] = arrived(v[h], flying[h], layers - 2, h)
@@ -171,7 +176,7 @@
     r0_copies = []
     s_far = sbuf[half_o, :]
     for c in range(2):
-        far = step_size * back_product(s_far, cw[j, c * cols:(c + 1) * cols, :])
+        far = step_size * back_product(s_far, cwt[j, :, c * cols:(c + 1) * cols])
         r0s[c] = (far + jnp.where(j == c, vbuf[half_o, :], 0.0)).astype(bf16)
         r0_copies.append(remote(r0s.at[c], r0r.at[c], rsend.at[c], rrecv.at[c], partner))
         r0_copies[c].start()
@@ -193,7 +198,7 @@
 
     s_near = sbuf[half_j, :]
     for c in range(2):
-        near = step_size * back_product(s_near, cw[j, c * cols:(c + 1) * cols, :])
+        near = step_size * back_product(s_near, cwt[j, :, c * cols:(c + 1) * cols])
         near = near + jnp.where(j == c, vbuf[half_j, :], 0.0)
         resid[c] = near - guess[0, half_j, c * cols:(c + 1) * cols].astype(f32)
     chain = [
@@ -221,6 +226,7 @@
         c_copy.wait_recv()
     cslopes[j] = slopes[0, half_j, :]
     cslopes[o] = slope_of(states[0, half_j, :], cw[o])
+    cwt[o] = cw[o].T
 
     @pl.when(not_top)
     def _():
@@ -232,7 +238,7 @@
             carried.append(inc[c].astype(f32))
             scaled_rows = (carried[c] * cslopes[c]).astype(bf16)
             for n in range(2):
-                block = cw[c, n * cols:(n + 1) * cols, :]
+                block = cwt[c, :, n * cols:(n + 1) * cols]
                 products[n] = products[n] + back_product(scaled_rows, block)
                 if c == 1:
                     total = carried[n] + layers * step_size * products[n] + resid[n]
@@ -332,6 +338,8 @@
                 pltpu.VMEM((layers, rows, width), bf16),
                 pltpu.VMEM((layers - 1, width, cols), bf16),
                 pltpu.VMEM((2, width, cols), bf16),
+                pltpu.VMEM((layers - 1, cols, width), bf16),
+                pltpu.VMEM((2, cols, width), bf16),
                 pltpu.VMEM((rows, cols), bf16),
                 pltpu.VMEM((layers, rows, cols), f32),
                 pltpu.VMEM((2, half, cols), f32),

time: 108 us -> 106 us (0.981)
  Pallas kernels: 107 us -> 105 us
    pallas_call x1, Pallas kernels: 102 us -> 100 us  [body(): pl.pallas_call(functools.partial(cycle, slab_count, dp_count, layers), ou...]
where the time goes in v4:
time: 106 us
  Pallas kernels  105 us (99%)
    pallas_call x1, Pallas kernels, body(): pl.pallas_call(functools.partial(cycle, slab_count, dp_count, layers), ou...  100 us
    pallas_call x1, Pallas kernels, body(): pl.pallas_call(weight_gradients, grid=(layers,), out_shape=(jax.ShapeDtyp...  4.8 us

profile of v4, /device:TPU:0, one launch (start us, length us, event | category | flops | bytes accessed | tf_op | source)
XLA Modules:
  0.0 105.7 jit_solution(5918401381698026879)
XLA Ops:
  0.6 100.3 %shard_map.59 = (bf16[4,128,512]{2,1,0:T(8,128)(2,1)}, bf16[4,256,512]{2,1,0:T(8,128)(2,1)}, bf16[4,256,512]{2,1,0:T(8,128)(2,1)}) custom-call(bf16[4,128,1024]{2,1,0:T(8,128)(2,1)} %states_in.1, bf16[4,512,512]{2,1,0:T(8,128)(2,1)} %weights.1, bf16[1,128,1024]{2,1,0:T(8,128)(2,1)} %guess.1, bf16[128,1024]{1,0:T(8,128)(2,1)} %cotangent.1), custom_call_target="tpu_custom_call" | custom-call | flops 3221225472 | bytes 8388608 | tf_op jit(solution)/shard_map/pallas_call | solution.py:328
  100.9 4.8 %shard_map.60 = (f32[4,512,512]{2,1,0:T(8,128)}, bf16[4,128,512]{2,1,0:T(8,128)(2,1)}) custom-call(bf16[4,256,512]{2,1,0:T(8,128)(2,1)} %get-tuple-element.7.inputs, bf16[4,256,512]{2,1,0:T(8,128)(2,1)} %get-tuple-element.8.scaled, bf16[4,128,512]{2,1,0:T(8,128)(2,1)} %get-tuple-element.9.adjoint_in), custom_call_target="tpu_custom_call" | custom-call | tf_op jit(solution)/shard_map/pallas_call | solution.py:381

commit v5 on v4

--- a/solution.py
+++ b/solution.py
@@ -16,6 +16,12 @@
     return jnp.dot(scaled_rows, turned_block, preferred_element_type=f32)
 
 
+def back_product_raw(scaled_rows, weight_block):
+    return lax.dot_general(
+        scaled_rows, weight_block, (((1,), (1,)), ((), ())), preferred_element_type=f32
+    )
+
+
 def slope_of(inputs, weight_block):
     tangent = jnp.tanh(jnp.dot(inputs, weight_block, preferred_element_type=f32))
     return 1.0 - tangent * tangent
@@ -24,10 +30,10 @@
 def cycle(
     slab_count, dp_count, layers,
     states_in, weights, guess, cotangent, adjoint, sg, stg,
-    states, gw, cw, wt, cwt, npt, slopes, cslopes, vbuf, sbuf, terminal,
-    exs, exr, r0s, r0r, resid, inc, oinc, ebuf, oe, sown,
+    states, gw, cw, wt, npt, slopes, cslopes, vbuf, sbuf, terminal,
+    exs, exr, r0s, r0r, resid, pair_slopes, pair_resid, errs, spread_errs, sown,
     wsend, wrecv, csend, crecv, lsem, osem, ssend, srecv, gsend, grecv,
-    xsend, xrecv, rsend, rrecv, psend, precv, nsend, nrecv, hsend, hrecv,
+    xsend, xrecv, rsend, rrecv, ksend, krecv, psend, precv, qsend, qrecv, nsend, nrecv, hsend, hrecv,
 ):
     slab, mine, j = lax.axis_index("layer"), lax.axis_index("dp"), lax.axis_index("mp")
     o = 1 - j
@@ -38,6 +44,12 @@
     to_peer = [lax.rem(mine + d, dp_count) for d in peers]
     from_peer = [lax.rem(mine + dp_count - d, dp_count) for d in peers]
     not_top, not_low = slab < slab_count - 1, slab > 0
+    core = lax.rem(slab, 2)
+    sibling = slab + 1 - 2 * core
+    pair_not_top, pair_not_low = slab < slab_count - 2, slab > 1
+    quarter = half // 2
+    keep = pl.ds(pl.multiple_of(core * quarter, quarter), quarter)
+    give = pl.ds(pl.multiple_of((1 - core) * quarter, quarter), quarter)
     own_in = pl.ds(pl.multiple_of(mine * blk, blk), blk)
     own_rows = pl.ds(pl.multiple_of(mine * rows, rows), rows)
     half_j = pl.ds(pl.multiple_of(j * half, half), half)
@@ -59,6 +71,16 @@
     for peer in to_peer:
         greet({"dp": peer})
     greet({"mp": o})
+    greet({"layer": sibling})
+    greet({"layer": sibling, "mp": o})
+
+    @pl.when(pair_not_top)
+    def _():
+        greet({"layer": slab + 2})
+
+    @pl.when(pair_not_low)
+    def _():
+        greet({"layer": slab - 2})
 
     @pl.when(not_top)
     def _():
@@ -68,17 +90,18 @@
     def _():
         greet({"layer": slab - 1})
 
-    pl.semaphore_wait(
-        barrier, dp_count + not_top.astype(jnp.int32) + not_low.astype(jnp.int32)
-    )
+    greeted = dp_count + 2
+    for there in (not_top, not_low, pair_not_top, pair_not_low):
+        greeted = greeted + there.astype(jnp.int32)
+    pl.semaphore_wait(barrier, greeted)
 
     states_copy = pltpu.make_async_copy(states_in, states, osem.at[0])
     states_copy.start()
 
     def home(layer):
-        return cw.at[j] if layer == 0 else gw.at[layer - 1]
-
-    partner = {"mp": o}
+        return cw.at[core, j] if layer == 0 else gw.at[layer - 1]
+
+    partner, twin = {"mp": o}, {"layer": sibling}
     point_copy = remote(guess.at[0, :, cols_j], npt, nsend.at[0], nrecv.at[0], {"layer": slab - 1})
 
     @pl.when(not_low)
@@ -92,15 +115,20 @@
     def piece_of(owner, n):
         return pl.ds(pl.multiple_of(owner * blk + n * piece, piece), piece)
 
-    c_copies = [remote(weights.at[0], cw.at[j, own_in], csend.at[0, 0], crecv.at[0, 0], partner)]
+    c_copies = [remote(weights.at[0], cw.at[core, j, own_in], csend.at[0, 0], crecv.at[0, 0], partner)]
     c_copies[0].start()
+    c_blocks = [own_in]
+    twin_copies = [
+        remote(weights.at[0], cw.at[core, j, own_in], ksend.at[0, 0, 0], krecv.at[0, 0, 0], twin)
+    ]
+    twin_copies[0].start()
     order = range(layers - 1, -1, -1)
     for layer in order:
         parts = pieces if layer == 0 else 1
         for n in range(parts):
             for d in peers:
                 source = weights.at[layer, n * piece:(n + 1) * piece] if layer == 0 else weights.at[layer]
-                target = cw.at[j, piece_of(mine, n)] if layer == 0 else home(layer).at[own_in]
+                target = cw.at[core, j, piece_of(mine, n)] if layer == 0 else home(layer).at[own_in]
                 sem = pieces - 1 + layer if layer else n
                 w_copies[layer, n, d] = remote(
                     source, target, wsend.at[sem, d - 1], wrecv.at[sem, d - 1],
@@ -156,19 +184,16 @@
             flying[h], term = fine_half(slot, h, layer, scaled_rows)
             v[h] = v[h] + term
     local_copies[0].wait()
-    cwt[j, :, own_in] = cw[j, own_in, :].T
     for n in range(pieces):
         for d in peers:
             w_copies[0, n, d].wait_recv()
-            block = cw.at[j, piece_of(from_peer[d - 1], n)]
+            c_blocks.append(piece_of(from_peer[d - 1], n))
+            block = cw.at[core, j, c_blocks[-1]]
             c_copies.append(remote(block, block, csend.at[d, n], crecv.at[d, n], partner))
             c_copies[-1].start()
-            if piece % 128 == 0:
-                landed = piece_of(from_peer[d - 1], n)
-                cwt[j, :, landed] = cw[j, landed, :].T
-    if piece % 128:
-        cwt[j] = cw[j].T
-    slopes[0] = slope_of(states[0], cw[j])
+            twin_copies.append(remote(block, block, ksend.at[0, d, n], krecv.at[0, d, n], twin))
+            twin_copies[-1].start()
+    slopes[0] = slope_of(states[0], cw[core, j])
     for h in range(2):
         v[h] = arrived(v[h], flying[h], layers - 2, h)
         vbuf[span[h], :] = v[h]
@@ -176,7 +201,7 @@
     r0_copies = []
     s_far = sbuf[half_o, :]
     for c in range(2):
-        far = step_size * back_product(s_far, cwt[j, :, c * cols:(c + 1) * cols])
+        far = step_size * back_product_raw(s_far, cw[core, j, c * cols:(c + 1) * cols, :])
         r0s[c] = (far + jnp.where(j == c, vbuf[half_o, :], 0.0)).astype(bf16)
         r0_copies.append(remote(r0s.at[c], r0r.at[c], rsend.at[c], rrecv.at[c], partner))
         r0_copies[c].start()
@@ -198,64 +223,96 @@
 
     s_near = sbuf[half_j, :]
     for c in range(2):
-        near = step_size * back_product(s_near, cwt[j, :, c * cols:(c + 1) * cols])
+        near = step_size * back_product_raw(s_near, cw[core, j, c * cols:(c + 1) * cols, :])
         near = near + jnp.where(j == c, vbuf[half_j, :], 0.0)
         resid[c] = near - guess[0, half_j, c * cols:(c + 1) * cols].astype(f32)
-    chain = [
-        remote(ebuf.at[c], inc.at[c], hsend.at[c], hrecv.at[c], {"layer": slab - 1})
-        for c in range(2)
-    ]
-
-    pass_on = remote(inc.at[o], oinc, psend.at[0], precv.at[0], partner)
-
-    @pl.when(jnp.logical_not(not_top))
-    def _():
-        inc[...] = jnp.zeros_like(inc)
-        pass_on.start()
-
     for c in range(2):
         r0_copies[c].wait_recv()
         resid[c] = resid[c] + r0r[c].astype(f32)
-
-        @pl.when(jnp.logical_not(not_top))
-        def _():
-            ebuf[c] = resid[c].astype(bf16)
-            chain[c].start()
-
-    for c_copy in c_copies:
+    pair_resid[core] = resid[:, keep, :]
+    twin_copies.append(
+        remote(resid.at[:, give], pair_resid.at[core], psend.at[0], precv.at[0], twin)
+    )
+    twin_copies[-1].start()
+    for n, (c_copy, block) in enumerate(zip(c_copies, c_blocks)):
         c_copy.wait_recv()
+        d, m = (0, 0) if n == 0 else (1 + (n - 1) % (dp_count - 1), (n - 1) // (dp_count - 1))
+        part = cw.at[core, o, block]
+        twin_copies.append(remote(part, part, ksend.at[1, d, m], krecv.at[1, d, m], twin))
+        twin_copies[-1].start()
     cslopes[j] = slopes[0, half_j, :]
-    cslopes[o] = slope_of(states[0, half_j, :], cw[o])
-    cwt[o] = cw[o].T
-
-    @pl.when(not_top)
-    def _():
+    cslopes[o] = slope_of(states[0, half_j, :], cw[core, o])
+    pair_slopes[core] = cslopes[:, keep, :]
+    twin_copies.append(
+        remote(cslopes.at[:, give], pair_slopes.at[core], psend.at[1], precv.at[1], twin)
+    )
+    twin_copies[-1].start()
+    for copy in twin_copies:
+        copy.wait_recv()
+
+    chain = [
+        remote(errs.at[2, n], errs.at[0, n], hsend.at[n], hrecv.at[n], {"layer": slab - 2})
+        for n in range(2)
+    ]
+
+    def coarse_step(parity, start, incoming=None, outgoing=None):
         carried, products = [], [0.0, 0.0]
         for c in range(2):
-            chain[c].wait_recv()
-            if c == 1:
-                pass_on.start()
-            carried.append(inc[c].astype(f32))
-            scaled_rows = (carried[c] * cslopes[c]).astype(bf16)
+            if incoming is not None:
+                incoming[c].wait_recv()
+            carried.append(errs[start, c].astype(f32))
+            scaled_rows = (carried[c] * pair_slopes[parity, c]).astype(bf16)
             for n in range(2):
-                block = cwt[c, :, n * cols:(n + 1) * cols]
-                products[n] = products[n] + back_product(scaled_rows, block)
+                block = cw[parity, c, n * cols:(n + 1) * cols, :]
+                products[n] = products[n] + back_product_raw(scaled_rows, block)
                 if c == 1:
-                    total = carried[n] + layers * step_size * products[n] + resid[n]
-                    ebuf[n] = total.astype(bf16)
-
-                    @pl.when(not_low)
-                    def _():
-                        chain[n].start()
-
-    e_copy = remote(ebuf.at[o], oe, psend.at[1], precv.at[1], partner)
-    e_copy.start()
-    pending += [pass_on, e_copy]
-
-    vbuf[half_j, :] = terminal[half_j, :] + inc[j].astype(f32)
-    pass_on.wait_recv()
-    vbuf[half_o, :] = terminal[half_o, :] + oinc[...].astype(f32)
-    v = [vbuf[span[h], :] for h in range(2)]
+                    total = carried[n] + layers * step_size * products[n] + pair_resid[parity, n]
+                    errs[start + 1, n] = total.astype(bf16)
+                    if outgoing is not None:
+
+                        @pl.when(pair_not_low)
+                        def _():
+                            outgoing[n].start()
+
+    @pl.when(jnp.logical_not(pair_not_top))
+    def _():
+        errs[0] = jnp.zeros(errs.shape[1:], bf16)
+        for n in range(2):
+            errs[1, n] = pair_resid[1, n].astype(bf16)
+
+    @pl.when(pair_not_top)
+    def _():
+        coarse_step(1, 0, incoming=chain)
+
+    place = 2 * j + core
+
+    def scatter(kind):
+        spread_errs[kind, place] = errs[1 - core + kind, j]
+        copies = []
+        for n, (index, c, device) in enumerate((
+            (core + kind, j, twin),
+            (1 - core + kind, o, partner),
+            (core + kind, o, {"layer": sibling, "mp": o}),
+        )):
+            copies.append(
+                remote(errs.at[index, c], spread_errs.at[kind, place], qsend.at[kind, n],
+                       qrecv.at[kind, n], device)
+            )
+            copies[-1].start()
+        return copies
+
+    in_copies = scatter(0)
+    coarse_step(0, 1, outgoing=chain)
+    own_copies = scatter(1)
+    pending += in_copies + own_copies
+
+    for copy in in_copies:
+        copy.wait_recv()
+    v = [
+        terminal[span[h], :]
+        + jnp.concatenate([spread_errs[0, 2 * h + t].astype(f32) for t in range(2)], 0)
+        for h in range(2)
+    ]
     flying = [None, None]
     g_copies = {}
 
@@ -285,21 +342,27 @@
                 flying[h], term = fine_half(slot, h, layer, scaled_rows)
                 v[h] = v[h] + term
         spread(layer)
-    e_copy.wait_recv()
-    adjoint[0, half_j, :] = (guess[0, half_j, cols_j].astype(f32) + ebuf[j].astype(f32)).astype(bf16)
-    adjoint[0, half_o, :] = (guess[0, half_o, cols_j].astype(f32) + oe[...].astype(f32)).astype(bf16)
+    for copy in own_copies:
+        copy.wait_recv()
+    for q in range(4):
+        lines = slice(q * quarter, (q + 1) * quarter)
+        own = guess[0, lines, cols_j].astype(f32) + spread_errs[1, q].astype(f32)
+        adjoint[0, lines, :] = own.astype(bf16)
     for copy in s_copies + list(g_copies.values()):
         copy.wait_recv()
     for copy in own_scaled + [own_states]:
         copy.wait()
-    for copy in pending + c_copies + s_copies + list(w_copies.values()) + list(g_copies.values()):
+    for copy in pending + c_copies + twin_copies + s_copies + list(w_copies.values()) + list(g_copies.values()):
         copy.wait_send()
 
     @pl.when(not_low)
     def _():
         point_copy.wait_send()
-        for c in range(2):
-            chain[c].wait_send()
+
+    @pl.when(pair_not_low)
+    def _():
+        for n in range(2):
+            chain[n].wait_send()
 
 
 def weight_gradients(inputs, scaled, adjoint_in, grads, adjoint):
@@ -320,7 +383,7 @@
         assert guess_points.shape[0] == 1
         half = rows // 2
         slots = 2 * (layers - 1)
-        assert slab_count > 1 and layers > 1 and blk % 64 == 0
+        assert slab_count % 2 == 0 and layers > 1 and blk % 64 == 0
         all_rows = rows * dp_count
         dma = pltpu.SemaphoreType.DMA
         vmem = pl.BlockSpec(memory_space=pltpu.VMEM)
@@ -337,9 +400,8 @@
             scratch_shapes=[
                 pltpu.VMEM((layers, rows, width), bf16),
                 pltpu.VMEM((layers - 1, width, cols), bf16),
-                pltpu.VMEM((2, width, cols), bf16),
+                pltpu.VMEM((2, 2, width, cols), bf16),
                 pltpu.VMEM((layers - 1, cols, width), bf16),
-                pltpu.VMEM((2, cols, width), bf16),
                 pltpu.VMEM((rows, cols), bf16),
                 pltpu.VMEM((layers, rows, cols), f32),
                 pltpu.VMEM((2, half, cols), f32),
@@ -351,10 +413,10 @@
                 pltpu.VMEM((2, half, cols), bf16),
                 pltpu.VMEM((2, half, cols), bf16),
                 pltpu.VMEM((2, half, cols), f32),
-                pltpu.VMEM((2, half, cols), bf16),
-                pltpu.VMEM((half, cols), bf16),
-                pltpu.VMEM((2, half, cols), bf16),
-                pltpu.VMEM((half, cols), bf16),
+                pltpu.VMEM((2, 2, half // 2, cols), f32),
+                pltpu.VMEM((2, 2, half // 2, cols), f32),
+                pltpu.VMEM((3, 2, half // 2, cols), bf16),
+                pltpu.VMEM((2, 4, half // 2, cols), bf16),
                 pltpu.VMEM((layers, rows, cols), bf16),
                 dma((layers + 3, dp_count - 1)), dma((layers + 3, dp_count - 1)),
                 dma((dp_count, 4)), dma((dp_count, 4)),
@@ -363,7 +425,9 @@
                 dma((layers, dp_count - 1)), dma((layers, dp_count - 1)),
                 dma((slots, 2)), dma((slots, 2)),
                 dma((2,)), dma((2,)),
+                dma((2, dp_count, 4)), dma((2, dp_count, 4)),
                 dma((2,)), dma((2,)),
+                dma((2, 3)), dma((2, 3)),
                 dma((1,)), dma((1,)),
                 dma((2,)), dma((2,)),
             ],

time: 106 us -> 104 us (0.981)
  Pallas kernels: 105 us -> 103 us
    pallas_call x1, Pallas kernels: 100 us -> 98.6 us  [body(): pl.pallas_call(functools.partial(cycle, slab_count, dp_count, layers), ou...]
where the time goes in v5:
time: 104 us
  Pallas kernels  103 us (99%)
    pallas_call x1, Pallas kernels, body(): pl.pallas_call(functools.partial(cycle, slab_count, dp_count, layers), ou...  98.6 us
    pallas_call x1, Pallas kernels, body(): pl.pallas_call(weight_gradients, grid=(layers,), out_shape=(jax.ShapeDtyp...  4.81 us

profile of v5, /device:TPU:0, one launch (start us, length us, event | category | flops | bytes accessed | tf_op | source)
XLA Modules:
  0.0 104.1 jit_solution(17217820458842617825)
XLA Ops:
  0.6 98.6 %shard_map.59 = (bf16[4,128,512]{2,1,0:T(8,128)(2,1)}, bf16[4,256,512]{2,1,0:T(8,128)(2,1)}, bf16[4,256,512]{2,1,0:T(8,128)(2,1)}) custom-call(bf16[4,128,1024]{2,1,0:T(8,128)(2,1)} %states_in.1, bf16[4,512,512]{2,1,0:T(8,128)(2,1)} %weights.1, bf16[1,128,1024]{2,1,0:T(8,128)(2,1)} %guess.1, bf16[128,1024]{1,0:T(8,128)(2,1)} %cotangent.1), custom_call_target="tpu_custom_call" | custom-call | flops 3221225472 | bytes 8388608 | tf_op jit(solution)/shard_map/pallas_call | solution.py:391
  99.3 4.8 %shard_map.60 = (f32[4,512,512]{2,1,0:T(8,128)}, bf16[4,128,512]{2,1,0:T(8,128)(2,1)}) custom-call(bf16[4,256,512]{2,1,0:T(8,128)(2,1)} %get-tuple-element.7.inputs, bf16[4,256,512]{2,1,0:T(8,128)(2,1)} %get-tuple-element.8.scaled, bf16[4,128,512]{2,1,0:T(8,128)(2,1)} %get-tuple-element.9.adjoint_in), custom_call_target="tpu_custom_call" | custom-call | tf_op jit(solution)/shard_map/pallas_call | solution.py:445

commit v6 on v5

--- a/solution.py
+++ b/solution.py
@@ -123,18 +123,29 @@
     ]
     twin_copies[0].start()
     order = range(layers - 1, -1, -1)
-    for layer in order:
-        parts = pieces if layer == 0 else 1
-        for n in range(parts):
+    stream = [(layer, n) for layer in order for n in range(pieces)]
+    for layer, n in stream:
+        for d in peers:
+            w_copies[layer, n, d] = remote(
+                weights.at[layer, n * piece:(n + 1) * piece],
+                home(layer).at[piece_of(mine, n)],
+                wsend.at[layer * pieces + n, d - 1], wrecv.at[layer * pieces + n, d - 1],
+                {"dp": to_peer[d - 1]},
+            )
+
+    def start_piece(index):
+        if index < len(stream):
             for d in peers:
-                source = weights.at[layer, n * piece:(n + 1) * piece] if layer == 0 else weights.at[layer]
-                target = cw.at[core, j, piece_of(mine, n)] if layer == 0 else home(layer).at[own_in]
-                sem = pieces - 1 + layer if layer else n
-                w_copies[layer, n, d] = remote(
-                    source, target, wsend.at[sem, d - 1], wrecv.at[sem, d - 1],
-                    {"dp": to_peer[d - 1]},
-                )
-                w_copies[layer, n, d].start()
+                w_copies[(*stream[index], d)].start()
+
+    def receive_piece(layer, n):
+        for d in peers:
+            w_copies[layer, n, d].wait_recv()
+        start_piece(stream.index((layer, n)) + window)
+
+    window = 5
+    for index in range(window):
+        start_piece(index)
     for layer in order:
         local_copies[layer] = pltpu.make_async_copy(
             weights.at[layer], home(layer).at[own_in], lsem.at[layer]
@@ -174,8 +185,8 @@
     states_copy.wait()
     for slot, layer in enumerate(range(layers - 1, 0, -1)):
         local_copies[layer].wait()
-        for d in peers:
-            w_copies[layer, 0, d].wait_recv()
+        for n in range(pieces):
+            receive_piece(layer, n)
         wt[layer - 1] = gw[layer - 1].T
         slopes[layer] = slope_of(states[layer], gw[layer - 1])
         for h in range(2):
@@ -185,8 +196,8 @@
             v[h] = v[h] + term
     local_copies[0].wait()
     for n in range(pieces):
+        receive_piece(0, n)
         for d in peers:
-            w_copies[0, n, d].wait_recv()
             c_blocks.append(piece_of(from_peer[d - 1], n))
             block = cw.at[core, j, c_blocks[-1]]
             c_copies.append(remote(block, block, csend.at[d, n], crecv.at[d, n], partner))
@@ -418,7 +429,7 @@
                 pltpu.VMEM((3, 2, half // 2, cols), bf16),
                 pltpu.VMEM((2, 4, half // 2, cols), bf16),
                 pltpu.VMEM((layers, rows, cols), bf16),
-                dma((layers + 3, dp_count - 1)), dma((layers + 3, dp_count - 1)),
+                dma((layers * 4, dp_count - 1)), dma((layers * 4, dp_count - 1)),
                 dma((dp_count, 4)), dma((dp_count, 4)),
                 dma((layers,)), dma((layers + 2,)),
                 dma((dp_count - 1,)), dma((dp_count - 1,)),

time: 104 us -> 104 us (level)
  no operation moved by 1% of the time
where the time goes in v6:
time: 104 us
  Pallas kernels  104 us (100%)
    pallas_call x1, Pallas kernels, body(): pl.pallas_call(functools.partial(cycle, slab_count, dp_count, layers), ou...  98.8 us
    pallas_call x1, Pallas kernels, body(): pl.pallas_call(weight_gradients, grid=(layers,), out_shape=(jax.ShapeDtyp...  4.8 us

profile of v6, /device:TPU:0, one launch (start us, length us, event | category | flops | bytes accessed | tf_op | source)
XLA Modules:
  0.0 104.3 jit_solution(6153020860746966753)
XLA Ops:
  0.6 98.8 %shard_map.59 = (bf16[4,128,512]{2,1,0:T(8,128)(2,1)}, bf16[4,256,512]{2,1,0:T(8,128)(2,1)}, bf16[4,256,512]{2,1,0:T(8,128)(2,1)}) custom-call(bf16[4,128,1024]{2,1,0:T(8,128)(2,1)} %states_in.1, bf16[4,512,512]{2,1,0:T(8,128)(2,1)} %weights.1, bf16[1,128,1024]{2,1,0:T(8,128)(2,1)} %guess.1, bf16[128,1024]{1,0:T(8,128)(2,1)} %cotangent.1), custom_call_target="tpu_custom_call" | custom-call | flops 3221225472 | bytes 8388608 | tf_op jit(solution)/shard_map/pallas_call | solution.py:402
  99.5 4.8 %shard_map.60 = (f32[4,512,512]{2,1,0:T(8,128)}, bf16[4,128,512]{2,1,0:T(8,128)(2,1)}) custom-call(bf16[4,256,512]{2,1,0:T(8,128)(2,1)} %get-tuple-element.7.inputs, bf16[4,256,512]{2,1,0:T(8,128)(2,1)} %get-tuple-element.8.scaled, bf16[4,128,512]{2,1,0:T(8,128)(2,1)} %get-tuple-element.9.adjoint_in), custom_call_target="tpu_custom_call" | custom-call | tf_op jit(solution)/shard_map/pallas_call | solution.py:456

commit v7 on v6

--- a/solution.py
+++ b/solution.py
@@ -312,10 +312,13 @@
             copies[-1].start()
         return copies
 
+    @pl.when(pair_not_low)
+    def _():
+        coarse_step(0, 1, outgoing=chain)
+
     in_copies = scatter(0)
-    coarse_step(0, 1, outgoing=chain)
-    own_copies = scatter(1)
-    pending += in_copies + own_copies
+    early = pending + c_copies + twin_copies + list(w_copies.values())
+    pending = list(in_copies)
 
     for copy in in_copies:
         copy.wait_recv()
@@ -353,6 +356,20 @@
                 flying[h], term = fine_half(slot, h, layer, scaled_rows)
                 v[h] = v[h] + term
         spread(layer)
+        if layer == layers - 1:
+            for copy in early[:len(early) // 2]:
+                copy.wait_send()
+        if layer == max(layers - 2, 1):
+            for copy in early[len(early) // 2:]:
+                copy.wait_send()
+        if layer == 1:
+
+            @pl.when(jnp.logical_not(pair_not_low))
+            def _():
+                coarse_step(0, 1)
+
+            own_copies = scatter(1)
+            pending += own_copies
     for copy in own_copies:
         copy.wait_recv()
     for q in range(4):
@@ -363,7 +380,7 @@
         copy.wait_recv()
     for copy in own_scaled + [own_states]:
         copy.wait()
-    for copy in pending + c_copies + twin_copies + s_copies + list(w_copies.values()) + list(g_copies.values()):
+    for copy in pending + s_copies + list(g_copies.values()):
         copy.wait_send()
 
     @pl.when(not_low)

time: 104 us -> 105 us (level)
  no operation moved by 1% of the time
where the time goes in v7:
time: 105 us; the launch traced here: 104 us
  Pallas kernels  104 us (99%)
    pallas_call x1, Pallas kernels, body(): pl.pallas_call(functools.partial(cycle, slab_count, dp_count, layers), ou...  98.9 us
    pallas_call x1, Pallas kernels, body(): pl.pallas_call(weight_gradients, grid=(layers,), out_shape=(jax.ShapeDtyp...  4.8 us

profile of v7, /device:TPU:0, one launch (start us, length us, event | category | flops | bytes accessed | tf_op | source)
XLA Modules:
  0.0 104.4 jit_solution(11770864498096544161)
XLA Ops:
  0.6 98.9 %shard_map.59 = (bf16[4,128,512]{2,1,0:T(8,128)(2,1)}, bf16[4,256,512]{2,1,0:T(8,128)(2,1)}, bf16[4,256,512]{2,1,0:T(8,128)(2,1)}) custom-call(bf16[4,128,1024]{2,1,0:T(8,128)(2,1)} %states_in.1, bf16[4,512,512]{2,1,0:T(8,128)(2,1)} %weights.1, bf16[1,128,1024]{2,1,0:T(8,128)(2,1)} %guess.1, bf16[128,1024]{1,0:T(8,128)(2,1)} %cotangent.1), custom_call_target="tpu_custom_call" | custom-call | flops 3221225472 | bytes 8388608 | tf_op jit(solution)/shard_map/pallas_call | solution.py:419
  99.6 4.8 %shard_map.60 = (f32[4,512,512]{2,1,0:T(8,128)}, bf16[4,128,512]{2,1,0:T(8,128)(2,1)}) custom-call(bf16[4,256,512]{2,1,0:T(8,128)(2,1)} %get-tuple-element.7.inputs, bf16[4,256,512]{2,1,0:T(8,128)(2,1)} %get-tuple-element.8.scaled, bf16[4,128,512]{2,1,0:T(8,128)(2,1)} %get-tuple-element.9.adjoint_in), custom_call_target="tpu_custom_call" | custom-call | tf_op jit(solution)/shard_map/pallas_call | solution.py:473

commit v8 on v7

--- a/solution.py
+++ b/solution.py
@@ -393,12 +393,34 @@
             chain[n].wait_send()
 
 
-def weight_gradients(inputs, scaled, adjoint_in, grads, adjoint):
-    product = lax.dot_general(
-        inputs[0], scaled[0], (((0,), (0,)), ((), ())), preferred_element_type=f32
-    )
-    grads[0] = step_size * product
-    adjoint[...] = adjoint_in[...]
+def weight_gradients(
+    layers, inputs, scaled, adjoint_in, grads, adjoint, inputs_buf, scaled_buf, grads_buf, sems
+):
+    order = range(layers - 1, -1, -1)
+    fetches = {}
+    for layer in order:
+        fetches[layer] = (
+            pltpu.make_async_copy(inputs.at[layer], inputs_buf.at[layer], sems.at[0, layer]),
+            pltpu.make_async_copy(scaled.at[layer], scaled_buf.at[layer], sems.at[1, layer]),
+        )
+        for copy in fetches[layer]:
+            copy.start()
+    stores = [pltpu.make_async_copy(adjoint_in, adjoint, sems.at[3, 0])]
+    stores[0].start()
+    for layer in order:
+        for copy in fetches[layer]:
+            copy.wait()
+        product = lax.dot_general(
+            inputs_buf[layer], scaled_buf[layer], (((0,), (0,)), ((), ())),
+            preferred_element_type=f32,
+        )
+        grads_buf[layer] = step_size * product
+        stores.append(
+            pltpu.make_async_copy(grads_buf.at[layer], grads.at[layer], sems.at[2, layer])
+        )
+        stores[-1].start()
+    for copy in stores:
+        copy.wait()
 
 
 def solution(mesh):
@@ -467,18 +489,20 @@
             ),
         )(states, weights, guess_points, cotangent)
 
-        def per_layer(*shape):
-            return pl.BlockSpec((1, *shape), lambda layer: (layer, 0, 0))
-
         grads, adjoint = pl.pallas_call(
-            weight_gradients,
-            grid=(layers,),
+            functools.partial(weight_gradients, layers),
             out_shape=(
                 jax.ShapeDtypeStruct((layers, blk, cols), f32),
                 jax.ShapeDtypeStruct((layers, rows, cols), bf16),
             ),
-            in_specs=[per_layer(all_rows, blk), per_layer(all_rows, cols), per_layer(rows, cols)],
-            out_specs=(per_layer(blk, cols), per_layer(rows, cols)),
+            in_specs=[anywhere] * 3,
+            out_specs=(anywhere, anywhere),
+            scratch_shapes=[
+                pltpu.VMEM((layers, all_rows, blk), bf16),
+                pltpu.VMEM((layers, all_rows, cols), bf16),
+                pltpu.VMEM((layers, blk, cols), f32),
+                dma((4, layers)),
+            ],
             compiler_params=pltpu.CompilerParams(vmem_limit_bytes=60 * 2**20),
         )(inputs, scaled, adjoint)
         return adjoint, grads

time: 105 us -> 117 us (1.11)
  Pallas kernels: 104 us -> 116 us
    pallas_call x1, Pallas kernels: 4.8 us -> 17.1 us  [body(): pl.pallas_call(functools.partial(weight_gradients, layers), out_shape=(ja...]
where the time goes in v8:
time: 117 us
  Pallas kernels  116 us (99%)
    pallas_call x1, Pallas kernels, body(): pl.pallas_call(functools.partial(cycle, slab_count, dp_count, layers), ou...  98.9 us
    pallas_call x1, Pallas kernels, body(): pl.pallas_call(functools.partial(weight_gradients, layers), out_shape=(ja...  17.1 us

profile of v8, /device:TPU:0, one launch (start us, length us, event | category | flops | bytes accessed | tf_op | source)
XLA Modules:
  0.0 116.7 jit_solution(6369572370842813252)
XLA Ops:
  0.6 98.9 %shard_map.59 = (bf16[4,128,512]{2,1,0:T(8,128)(2,1)}, bf16[4,256,512]{2,1,0:T(8,128)(2,1)}, bf16[4,256,512]{2,1,0:T(8,128)(2,1)}) custom-call(bf16[4,128,1024]{2,1,0:T(8,128)(2,1)} %states_in.1, bf16[4,512,512]{2,1,0:T(8,128)(2,1)} %weights.1, bf16[1,128,1024]{2,1,0:T(8,128)(2,1)} %guess.1, bf16[128,1024]{1,0:T(8,128)(2,1)} %cotangent.1), custom_call_target="tpu_custom_call" | custom-call | flops 3221225472 | bytes 8388608 | tf_op jit(solution)/shard_map/pallas_call | solution.py:441
  99.6 17.1 %shard_map.60 = (f32[4,512,512]{2,1,0:T(8,128)}, bf16[4,128,512]{2,1,0:T(8,128)(2,1)}) custom-call(bf16[4,256,512]{2,1,0:T(8,128)(2,1)} %get-tuple-element.7.inputs, bf16[4,256,512]{2,1,0:T(8,128)(2,1)} %get-tuple-element.8.scaled, bf16[4,128,512]{2,1,0:T(8,128)(2,1)} %get-tuple-element.9.adjoint_in), custom_call_target="tpu_custom_call" | custom-call | tf_op jit(solution)/shard_map/pallas_call | solution.py:492

commit v9 on v8

--- a/solution.py
+++ b/solution.py
@@ -222,13 +222,13 @@
     for d in peers:
         block = pl.ds(pl.multiple_of(to_peer[d - 1] * blk, blk), blk)
         s_copies.append(
-            remote(states_in.at[:, :, block], stg.at[:, own_rows, :], ssend.at[d - 1],
+            remote(states.at[:, :, block], stg.at[:, own_rows, :], ssend.at[d - 1],
                    srecv.at[d - 1], {"dp": to_peer[d - 1]})
         )
         s_copies[-1].start()
 
     own_states = pltpu.make_async_copy(
-        states_in.at[:, :, own_in], stg.at[:, own_rows, :], osem.at[1]
+        states.at[:, :, own_in], stg.at[:, own_rows, :], osem.at[1]
     )
     own_states.start()
 
@@ -405,8 +405,8 @@
         )
         for copy in fetches[layer]:
             copy.start()
-    stores = [pltpu.make_async_copy(adjoint_in, adjoint, sems.at[3, 0])]
-    stores[0].start()
+    stores = []
+    adjoint[...] = adjoint_in[...]
     for layer in order:
         for copy in fetches[layer]:
             copy.wait()
@@ -495,13 +495,13 @@
                 jax.ShapeDtypeStruct((layers, blk, cols), f32),
                 jax.ShapeDtypeStruct((layers, rows, cols), bf16),
             ),
-            in_specs=[anywhere] * 3,
-            out_specs=(anywhere, anywhere),
+            in_specs=[anywhere, anywhere, vmem],
+            out_specs=(anywhere, vmem),
             scratch_shapes=[
                 pltpu.VMEM((layers, all_rows, blk), bf16),
                 pltpu.VMEM((layers, all_rows, cols), bf16),
                 pltpu.VMEM((layers, blk, cols), f32),
-                dma((4, layers)),
+                dma((3, layers)),
             ],
             compiler_params=pltpu.CompilerParams(vmem_limit_bytes=60 * 2**20),
         )(inputs, scaled, adjoint)

time: 117 us -> 105 us (0.90)
  Pallas kernels: 116 us -> 104 us
    pallas_call x1, Pallas kernels: 17.1 us -> 5.3 us  [body(): pl.pallas_call(functools.partial(weight_gradients, layers), out_shape=(ja...]
where the time goes in v9:
time: 105 us
  Pallas kernels  104 us (99%)
    pallas_call x1, Pallas kernels, body(): pl.pallas_call(functools.partial(cycle, slab_count, dp_count, layers), ou...  98.8 us
    pallas_call x1, Pallas kernels, body(): pl.pallas_call(functools.partial(weight_gradients, layers), out_shape=(ja...  5.3 us

profile of v9, /device:TPU:0, one launch (start us, length us, event | category | flops | bytes accessed | tf_op | source)
XLA Modules:
  0.0 104.7 jit_solution(11798634234416659537)
XLA Ops:
  0.6 98.8 %shard_map.59 = (bf16[4,128,512]{2,1,0:T(8,128)(2,1)}, bf16[4,256,512]{2,1,0:T(8,128)(2,1)}, bf16[4,256,512]{2,1,0:T(8,128)(2,1)}) custom-call(bf16[4,128,1024]{2,1,0:T(8,128)(2,1)} %states_in.1, bf16[4,512,512]{2,1,0:T(8,128)(2,1)} %weights.1, bf16[1,128,1024]{2,1,0:T(8,128)(2,1)} %guess.1, bf16[128,1024]{1,0:T(8,128)(2,1)} %cotangent.1), custom_call_target="tpu_custom_call" | custom-call | flops 3221225472 | bytes 8388608 | tf_op jit(solution)/shard_map/pallas_call | solution.py:441
  99.4 5.3 %shard_map.60 = (f32[4,512,512]{2,1,0:T(8,128)}, bf16[4,128,512]{2,1,0:T(8,128)(2,1)}) custom-call(bf16[4,256,512]{2,1,0:T(8,128)(2,1)} %get-tuple-element.7.inputs, bf16[4,256,512]{2,1,0:T(8,128)(2,1)} %get-tuple-element.8.scaled, bf16[4,128,512]{2,1,0:T(8,128)(2,1)} %get-tuple-element.9.adjoint_in), custom_call_target="tpu_custom_call" | custom-call | tf_op jit(solution)/shard_map/pallas_call | solution.py:492
